TPU v7x, 128 devices: a whole 4x4x4 slice. The times are simulated.
128 devices in a mesh: ctx: 8 (over x_hi, y), exp: 16 (over z, x_lo, core).
Axes of the slice: x: 4 (x_hi: 2, x_lo: 2; x = x_hi * 2 + x_lo), y: 4, z: 4, core: 2. Of those that a mesh axis runs over, the one named last changes fastest.
Arguments:
- hidden_in: bfloat16 [16384, 2048], P(('ctx', 'exp')), may hold values from -6 to 6
- attn_gain: float32 [2048], replicated, may hold values from 0.1 to 1.9
- w_query: bfloat16 [2048, 2048], P(None, 'exp'), may hold values from -0.125 to 0.125
- w_key: bfloat16 [2048, 256], replicated, may hold values from -0.125 to 0.125
- w_value: bfloat16 [2048, 256], replicated, may hold values from -0.125 to 0.125
- q_gain: float32 [128], replicated, may hold values from 1.4 to 10
- k_gain: float32 [128], replicated, may hold values from 1.4 to 10
- w_out: bfloat16 [2048, 2048], P('exp'), may hold values from -0.125 to 0.125
- ffn_gain: float32 [2048], replicated, may hold values from 0.1 to 1.9
- w_gate: bfloat16 [128, 2048, 768], P(('ctx', 'exp')), may hold values from -0.125 to 0.125
- w_up: bfloat16 [128, 2048, 768], P(('ctx', 'exp')), may hold values from -0.125 to 0.125
- w_down: bfloat16 [128, 768, 2048], P(('ctx', 'exp')), may hold values from -0.21875 to 0.21875
- expert_ids: int32 [16384, 8], P(('ctx', 'exp')), may hold values from 0 to 127, all different within a row; in each aligned block of 128 rows (0 to 127, 128 to 255, ...) at most 10 rows name the same one
- gate_weights: float32 [16384, 8], P(('ctx', 'exp')), may hold values from 0.05 to 1
Outputs:
- layer_out: bfloat16 [16384, 2048], P(('ctx', 'exp'))
Inputs may be any that keep to these rules, and one draw needn't show every extreme that they name: `expert_ids`: each row names 8 different experts. Among the rows of one device no expert is named more than 10 times, and in every draw some expert is named exactly 10 times by the rows of some device.
All inputs are finite; a program needn't handle non-finite values.
Results may differ from a plain program's by a relative error of at most 0.023.
The roundings to bfloat16 on the way count: a program that leaves them out, or rounds other values in their place, can miss the bound.
Values may be sent and summed in bfloat16 or wider, within the bound.
A program may use at most 128 MiB of HBM per device.

v0:
```python
import math

import jax
import jax.numpy as jnp
from jax import lax
from jax.sharding import PartitionSpec as P

TOPK = 8
HEADS = 16
KVH = 2


epsilon = 1e-06
rope_base = 1000000.0


def rms_scale(values, gains):
    return values * lax.rsqrt(jnp.mean(values * values, axis=-1, keepdims=True) + epsilon) * gains


def rotate(values, places):
    half_dim = values.shape[-1] // 2
    frequency = jnp.exp(
        jnp.arange(half_dim, dtype=jnp.float32) * (-2.0 * math.log(rope_base) / values.shape[-1])
    )
    angles = places.astype(jnp.float32)[:, None] * frequency[None, :]
    cosine = jnp.cos(angles)[:, None, :]
    sine_part = jnp.sin(angles)[:, None, :]
    first_part = values[..., :half_dim]
    second_part = values[..., half_dim:]
    return jnp.concatenate(
        [
            first_part * cosine - second_part * sine_part,
            second_part * cosine + first_part * sine_part,
        ],
        axis=-1,
    )


def token_place(row_ids, ctx_of, half_rows):
    half_idx = row_ids // half_rows
    offset = row_ids % half_rows
    segment = 2 * ctx_of + half_idx
    return segment * half_rows + offset


def on_device(
    hidden_in,
    attn_gain,
    w_query,
    w_key,
    w_value,
    q_gain,
    k_gain,
    w_out,
    ffn_gain,
    w_gate,
    w_up,
    w_down,
    expert_ids,
    gate_weights,
):
    head_dim = q_gain.shape[0]
    tok_rows = hidden_in.shape[0]
    model_width = hidden_in.shape[1]
    ctx_count = lax.axis_size("ctx")
    exp_count = lax.axis_size("exp")
    ctx_index = lax.axis_index("ctx")
    exp_index = lax.axis_index("exp")
    block_rows = tok_rows * exp_count
    half_rows = block_rows // 2
    heads_here = w_query.shape[1] // head_dim
    normed = rms_scale(hidden_in.astype(jnp.float32), attn_gain).astype(jnp.bfloat16)
    kv_column = exp_index * heads_here // (HEADS // KVH) * head_dim
    key_cols = lax.dynamic_slice_in_dim(w_key, kv_column, head_dim, 1)
    value_cols = lax.dynamic_slice_in_dim(w_value, kv_column, head_dim, 1)
    w_joined = jnp.concatenate([w_query, key_cols, value_cols], axis=1)
    query_width = heads_here * head_dim
    row_piece = lax.all_gather(normed, "exp", axis=0, tiled=True)
    projected = jnp.dot(row_piece, w_joined, preferred_element_type=jnp.float32)
    row_ids = jnp.arange(row_piece.shape[0], dtype=jnp.int32)
    places = token_place(row_ids, ctx_index, half_rows)
    queries = rotate(
        rms_scale(projected[:, :query_width].reshape(-1, heads_here, head_dim), q_gain), places
    )
    key_part = rotate(
        rms_scale(projected[:, query_width : query_width + head_dim][:, None, :], k_gain), places
    )[:, 0]
    value_part = projected[:, query_width + head_dim :]
    joined = jnp.concatenate(
        [queries.reshape(-1, query_width), key_part, value_part], axis=1
    ).astype(jnp.bfloat16)
    queries = joined[:, :query_width].reshape(block_rows, heads_here, head_dim)
    key_rows = joined[:, query_width : query_width + head_dim]
    value_rows = joined[:, query_width + head_dim :]
    query_places = token_place(jnp.arange(block_rows, dtype=jnp.int32), ctx_index, half_rows)
    query_halves = (queries[:half_rows], queries[half_rows:])
    place_halves = (query_places[:half_rows], query_places[half_rows:])
    score_scale = 1.0 / math.sqrt(head_dim)
    start_state = (
        jnp.full((heads_here, half_rows), -1e30, jnp.float32),
        jnp.zeros((heads_here, half_rows), jnp.float32),
        jnp.zeros((half_rows, heads_here, head_dim), jnp.float32),
    )
    key_block = lax.all_gather(key_rows, "ctx", axis=0, tiled=True)
    value_block = lax.all_gather(value_rows, "ctx", axis=0, tiled=True)
    piece_len = key_block.shape[0]
    tile_len = math.gcd(piece_len, 1024)

    def visit_tile(tile_idx, state):
        key_tile = lax.dynamic_slice_in_dim(key_block, tile_idx * tile_len, tile_len, 0)
        value_tile = lax.dynamic_slice_in_dim(value_block, tile_idx * tile_len, tile_len, 0)
        key_ids = tile_idx * tile_len + jnp.arange(tile_len, dtype=jnp.int32)
        key_places = token_place(key_ids % block_rows, key_ids // block_rows, half_rows)
        renewed = []
        for query_half, place_half, running in zip(query_halves, place_halves, state):

            def update(current, query_half=query_half, place_half=place_half):
                run_max, run_sum, run_out = current
                scores = (
                    jnp.einsum(
                        "qhd,kd->hqk", query_half, key_tile, preferred_element_type=jnp.float32
                    )
                    * score_scale
                )
                visible = key_places[None, None, :] <= place_half[None, :, None]
                row_top = jnp.max(jnp.where(visible, scores, -jnp.inf), axis=2)
                new_max = jnp.maximum(run_max, row_top)
                exp_weights = jnp.where(visible, jnp.exp(scores - new_max[:, :, None]), 0.0)
                rescale = jnp.exp(run_max - new_max)
                new_sum = run_sum * rescale + jnp.sum(exp_weights, axis=2)
                new_out = run_out * rescale.T[:, :, None] + jnp.einsum(
                    "hqk,kd->qhd",
                    exp_weights.astype(jnp.bfloat16),
                    value_tile,
                    preferred_element_type=jnp.float32,
                )
                return (new_max, new_sum, new_out)

            def keep_state(current):
                return current

            renewed.append(
                lax.cond(jnp.min(key_places) <= jnp.max(place_half), update, keep_state, running)
            )
        return tuple(renewed)

    final_state = lax.fori_loop(0, piece_len // tile_len, visit_tile, (start_state, start_state))
    halves_out = []
    for run_max, run_sum, run_out in final_state:
        halves_out.append(
            (run_out / run_sum.T[:, :, None]).astype(jnp.bfloat16).reshape(half_rows, query_width)
        )
    attended = jnp.concatenate(halves_out, axis=0)
    projected_out = lax.psum_scatter(
        jnp.dot(attended, w_out, preferred_element_type=jnp.float32).astype(jnp.bfloat16),
        "exp",
        scatter_dimension=0,
        tiled=True,
    ).astype(jnp.float32)
    resid = (hidden_in.astype(jnp.float32) + projected_out).astype(jnp.bfloat16)
    normed_ffn = rms_scale(resid.astype(jnp.float32), ffn_gain).astype(jnp.bfloat16)
    local_experts = w_gate.shape[0]
    device_count = ctx_count * exp_count
    experts_all = local_experts * device_count
    capacity = tok_rows * TOPK * 5 // (4 * experts_all)
    flat_ids = expert_ids.reshape(-1)
    count_rows = flat_ids.shape[0]
    matches = flat_ids[:, None] == jnp.arange(experts_all, dtype=jnp.int32)[None, :]
    row_range = jnp.arange(count_rows, dtype=jnp.int32)
    earlier = (row_range[:, None] > row_range[None, :]).astype(jnp.bfloat16)
    before = jnp.dot(earlier, matches.astype(jnp.bfloat16), preferred_element_type=jnp.float32)
    slot_rank = jnp.sum(jnp.where(matches, before, 0.0), axis=1).astype(jnp.int32)
    slot_index = flat_ids * capacity + slot_rank
    slot_table = (
        jnp.full((experts_all * capacity,), tok_rows, jnp.int32)
        .at[slot_index]
        .set(row_range // TOPK)
    )
    padded_rows = jnp.concatenate([normed_ffn, jnp.zeros((1, model_width), jnp.bfloat16)], axis=0)
    outgoing = padded_rows[slot_table].reshape(device_count, local_experts, capacity, model_width)
    arrived = lax.all_to_all(outgoing, ("ctx", "exp"), split_axis=0, concat_axis=0, tiled=True)
    rows_in = arrived[:, 0].reshape(-1, model_width)
    gate_out = jnp.dot(rows_in, w_gate[0], preferred_element_type=jnp.float32)
    up_out = jnp.dot(rows_in, w_up[0], preferred_element_type=jnp.float32)
    inner_act = (jax.nn.silu(gate_out) * up_out).astype(jnp.bfloat16)
    answer = jnp.dot(inner_act, w_down[0], preferred_element_type=jnp.float32).astype(jnp.bfloat16)
    results = [answer.reshape(arrived.shape[0], arrived.shape[2], model_width)]
    returned = lax.all_to_all(
        jnp.stack(results, axis=1), ("ctx", "exp"), split_axis=0, concat_axis=0, tiled=True
    )
    flat_back = returned.reshape(experts_all * capacity, model_width)
    picked = flat_back[slot_index].astype(jnp.float32).reshape(tok_rows, TOPK, model_width)
    shares = gate_weights / jnp.sum(gate_weights, axis=1, keepdims=True)
    mixture = jnp.sum(shares[:, :, None] * picked, axis=1)
    return (resid.astype(jnp.float32) + mixture).astype(jnp.bfloat16)


def solution(mesh):
    placed = (
        P(("ctx", "exp"), None),
        P(),
        P(None, "exp"),
        P(),
        P(),
        P(),
        P(),
        P("exp", None),
        P(),
        P(("ctx", "exp"), None, None),
        P(("ctx", "exp"), None, None),
        P(("ctx", "exp"), None, None),
        P(("ctx", "exp"), None),
        P(("ctx", "exp"), None),
    )
    return jax.shard_map(
        on_device, mesh=mesh, in_specs=placed, out_specs=P(("ctx", "exp"), None), check_vma=False
    )
```

profile of v0, /device:TPU:0, one launch (start us, length us, event | category | flops | bytes accessed | tf_op | source)
XLA Modules:
  0.0 915.5 jit_solution(10228791216584226625)
XLA Ops:
  7.9 2.0 fusion.67
  10.1 2.3 constant_dynamic-slice_fusion.2
  12.4 52.4 %all-gather.5.cloned.1.call-done = bf16[2048,2048]{1,0:T(8,128)(2,1)} async-done(((bf16[128,2048]{1,0:T(8,128)(2,1)}), bf16[2048,2048]{1,0:T(8,128)(2,1)}) %all-gather.5.cloned.1.call-update) | async-done | bytes 8388624 | tf_op jit(solution)/shard_map/all_gather | solution.py:79
  64.8 6.3 fusion.57
  71.6 3.1 fusion.88
  75.7 2.1 slice.92
  78.8 1.8 pad_maximum_fusion.1
  83.2 64.8 %all-gather.9.cloned.1.call-done = bf16[16384,1,128]{0,2,1:T(8,128)(2,1)} async-done(((bf16[2048,1,128]{0,2,1:T(8,128)(2,1)}), bf16[16384,1,128]{0,2,1:T(8,128)(2,1)}) %all-gather.9.cloned.1.call-update) | async-done | bytes 4194320 | tf_op jit(solution)/shard_map/all_gather | solution.py:105
  148.0 71.5 %all-gather.7.cloned.1.call-done = bf16[16384,128]{0,1:T(8,128)(2,1)} async-done(((bf16[2048,128]{0,1:T(8,128)(2,1)}), bf16[16384,128]{0,1:T(8,128)(2,1)}) %all-gather.7.cloned.1.call-update) | async-done | bytes 4194320 | tf_op jit(solution)/shard_map/all_gather | solution.py:106
  221.3 133.1 %while.26 = (s32[]{:T(128)}, f32[1,1024]{1,0:T(1,128)S(1)}, f32[1,1024]{1,0:T(1,128)S(1)}, f32[1024,1,128]{2,0,1:T(8,128)}, f32[1,1024]{1,0:T(1,128)S(1)}, /*ind...) while((s32[]{:T(128)}, f32[1,1024]{1,0:T(1,128)S(1)}, ...), condition=%wide.region_15.16_spmd, body=%wide.region_5.15_spmd.sunk | while | flops 1103675392 | bytes 41603736 | solution.py:148
  227.5 5.1 conditional.5
  227.6 1.8 fusion.18
  233.7 5.0 conditional.4
  233.8 1.8 fusion
  245.0 5.1 conditional.5
  245.0 1.8 fusion.18
  356.9 6.6 convolution_convert_fusion.1
  365.3 4.5 scatter_custom_fusion
  369.8 230.1 %reduce-scatter.2.cloned.1.call-done = bf16[128,2048]{1,0:T(8,128)(2,1)} async-done(((bf16[2048,2048]{1,0:T(8,128)(2,1)}), bf16[128,2048]{1,0:T(8,128)(2,1)}) %reduce-scatter.2.cloned.1.call-update) | async-done | bytes 524304 | tf_op jit(solution)/shard_map/reduce_scatter | solution.py:155
  603.7 12.0 %gather_fusion = bf16[1280,2048]{1,0:T(8,128)(2,1)} fusion(bf16[129,2048]{1,0:T(8,128)(2,1)} %concatenate.23, s32[2048]{0:T(1024)S(1)} %pad_clamp_fusion), kind=kCustom, calls=%fused_computation | custom fusion | bytes 10490880 | tf_op jit(solution)/shard_map/gather | solution.py:181
  615.7 9.6 %reshape.368 = bf16[128,1,10,2048]{3,2,0,1:T(8,128)(2,1)} reshape(bf16[1280,2048]{1,0:T(8,128)(2,1)} %gather_fusion) | data formatting | bytes 10485760 | tf_op jit(solution)/shard_map/reshape | solution.py:181
  625.2 105.2 %all_to_all.10 = bf16[128,1,10,2048]{3,2,1,0:T(8,128)(2,1)} all-to-all(bf16[128,1,10,2048]{3,2,1,0:T(8,128)(2,1)} %bitcast.125), channel_id=1, replica_groups=mesh['ctx'=8,'exp'=16] {'ctx','exp'}, dimensions={0} | all-to-all | bytes 10485760 | tf_op jit(solution)/shard_map/all_to_all | solution.py:182
  730.4 9.8 %reshape_squeeze.3 = bf16[1280,2048]{1,0:T(8,128)(2,1)} reshape(bf16[128,1,10,2048]{3,2,1,0:T(8,128)(2,1)} %all_to_all.10) | data formatting | bytes 10485760 | tf_op jit(solution)/shard_map/reshape;squeeze | solution.py:183
  740.3 7.2 fusion.55
  747.5 4.8 fusion.52
  752.4 6.0 convolution_convert_fusion
  758.4 9.5 %stack_reshape.3 = bf16[128,1,10,2048]{3,2,0,1:T(8,128)(2,1)} reshape(bf16[1280,2048]{1,0:T(8,128)(2,1)} %convolution_convert_fusion) | data formatting | bytes 10485760 | tf_op jit(solution)/shard_map/stack;reshape | solution.py:190
  767.9 9.2 %all-to-all-start.1 = ((bf16[128,1,10,2048]{3,2,1,0:T(8,128)(2,1)}), bf16[128,1,10,2048]{3,2,1,0:T(8,128)(2,1)}, u32[]{:S(2)}, u32[]{:S(2)}) async-start(bf16[128,1,10,2048]{3,2,1,0:T(8,128)(2,1)} %bitcast.124), calls=%async_computation.2 | async-start | bytes 16777216 | tf_op jit(solution)/shard_map/all_to_all | solution.py:189
  777.3 102.3 %all-to-all-done.1 = bf16[128,1,10,2048]{3,2,1,0:T(8,128)(2,1)} async-done(((bf16[128,1,10,2048]{3,2,1,0:T(8,128)(2,1)}), bf16[128,1,10,2048]{3,2,1,0:T(8,128)(2,1)}, u32[]{:S(2)}, u32[]{:S(2)}) %all-to-all-start.1) | async-done | bytes 5242912 | tf_op jit(solution)/shard_map/all_to_all | solution.py:189
  879.6 9.8 %reshape.369 = bf16[1280,2048]{1,0:T(8,128)(2,1)} reshape(bf16[128,1,10,2048]{3,2,1,0:T(8,128)(2,1)} %all-to-all-done.1) | data formatting | bytes 10485760 | tf_op jit(solution)/shard_map/reshape | solution.py:192
  889.4 12.0 %gather_fusion.1 = bf16[1024,2048]{1,0:T(8,128)(2,1)} fusion(bf16[1280,2048]{1,0:T(8,128)(2,1)} %reshape.369, s32[1024]{0:T(1024)S(1)} %broadcast_clamp_fusion), kind=kCustom, calls=%fused_computation.1 | custom fusion | bytes 8392704 | tf_op jit(solution)/shard_map/gather | solution.py:193
  901.4 6.6 fusion.50
  (196 shorter events, 107.3 us)
Async XLA Ops:
  6.5 745.8 %copy-start = (bf16[1,768,2048]{2,1,0:T(8,128)(2,1)S(1)}, bf16[1,768,2048]{2,1,0:T(8,128)(2,1)}, u32[]{:S(2)}) copy-start(bf16[1,768,2048]{2,1,0:T(8,128)(2,1)} %param.31) | copy-start | bytes 9437188
  6.5 58.2 %all-gather.5.cloned.1.call-start = ((), (), s32[]{:S(2)}) async-start(), calls=%async_computation.3 | async-start | bytes 8912896 | tf_op jit(solution)/shard_map/all_gather | solution.py:79
  10.0 138.1 %all-gather.9.cloned.1.call-start = ((), (), s32[]{:S(2)}) async-start(), calls=%async_computation.6 | async-start | bytes 4718592 | tf_op jit(solution)/shard_map/all_gather | solution.py:105
  64.8 6.6 copy-start.14
  64.8 6.6 copy-start.15
  71.1 3.6 copy-start.2
  75.6 144.0 %all-gather.7.cloned.1.call-start = ((), (), s32[]{:S(2)}) async-start(), calls=%async_computation.4 | async-start | bytes 4718592 | tf_op jit(solution)/shard_map/all_gather | solution.py:106
  77.8 522.1 %reduce-scatter.2.cloned.1.call-start = ((), (), s32[]{:S(2)}) async-start(), calls=%async_computation.5 | async-start | bytes 8912896 | tf_op jit(solution)/shard_map/reduce_scatter | solution.py:155
  227.5 2.9 copy-start.3
  227.6 2.9 copy-start.9
  231.8 0.8 copy-start.10
  233.8 2.9 copy-start.4
  233.8 2.9 copy-start.7
  238.0 0.8 copy-start.8
  245.0 2.9 copy-start.3
  245.0 2.9 copy-start.9
  249.2 0.8 copy-start.10
  363.5 0.7 copy-start.11
  363.5 237.9 %copy-start.13 = (f32[2048]{0:T(1024)S(1)}, f32[2048]{0:T(1024)}, u32[]{:S(2)}) copy-start(f32[2048]{0:T(1024)} %param.28) | copy-start | bytes 24580
  740.3 7.3 copy-start.5
  740.3 7.3 copy-start.16
  767.9 9.2 %copy-start.12 = (f32[128,8]{0,1:T(8,128)S(1)}, f32[128,8]{0,1:T(8,128)}, u32[]{:S(2)}) copy-start(f32[128,8]{0,1:T(8,128)} %param.33) | copy-start | bytes 12292
  767.9 111.6 %all-to-all-start.1 = ((bf16[128,1,10,2048]{3,2,1,0:T(8,128)(2,1)}), bf16[128,1,10,2048]{3,2,1,0:T(8,128)(2,1)}, u32[]{:S(2)}, u32[]{:S(2)}) async-start(bf16[128,1,10,2048]{3,2,1,0:T(8,128)(2,1)} %bitcast.124), calls=%async_computation.2 | async-start | bytes 16777216 | tf_op jit(solution)/shard_map/all_to_all | solution.py:189
  901.4 6.6 copy-start.1
  901.4 6.6 copy-start.6
Sparse Core Ops, SparseCore 0:
  10.1 54.6 all-gather.4
  75.7 72.2 all-gather.8
  150.3 69.1 all-gather.6
  363.7 236.1 reduce-scatter.1
where the time goes:
time: 923 us; the launch traced here: 916 us
  waiting for transfers between devices  521 us (56%)
  local copies, waits for them, and re-layouts  151 us (16%)
  blocking collectives  105 us (11%)
  matrix products  41.1 us (4%)
  loops' own time  38 us (4%)
  other arithmetic  36.3 us (4%)
  between operations  13.4 us (1%)
  starting transfers between devices  9.49 us (1%)
    reduce_scatter x1, waiting for transfers between devices, on_device(): lax.psum_scatter(jnp.dot(attended, w_out, preferred_element_type=jnp.floa...  230 us
    all_to_all x1, blocking collectives, on_device(): lax.all_to_all(outgoing, ('ctx', 'exp'), split_axis=0, concat_axis=0, til...  105 us
    all_to_all x1, waiting for transfers between devices, on_device(): lax.all_to_all(jnp.stack(results, axis=1), ('ctx', 'exp'), split_axis=0,...  102 us
    all_gather x1, waiting for transfers between devices, on_device(): value_block = lax.all_gather(value_rows, 'ctx', axis=0, tiled=True)  71.5 us
    all_gather x1, waiting for transfers between devices, on_device(): key_block = lax.all_gather(key_rows, 'ctx', axis=0, tiled=True)  64.8 us
    all_gather x1, waiting for transfers between devices, on_device(): row_piece = lax.all_gather(normed, 'exp', axis=0, tiled=True)  52.4 us
    dynamic_slice x32, local copies, waits for them, and re-layouts, visit_tile(): lax.dynamic_slice_in_dim(value_block, tile_idx * tile_len, tile_len, 0)  41.7 us
    another operation x1, loops' own time, on_device(): lax.fori_loop(0, piece_len // tile_len, visit_tile, (start_state, start_s...  37.3 us
  transfers between devices with their start and end apart: 5, of which 5 were waited for; matrix products, arithmetic and copies ran while one was open for 2% of the time, Pallas kernels for 0%

commit v1 on v0

--- a/solution.py
+++ b/solution.py
@@ -1,13 +1,216 @@
+import functools
 import math
 
 import jax
 import jax.numpy as jnp
 from jax import lax
+from jax.experimental import pallas as pl
+from jax.experimental.pallas import tpu as pltpu
 from jax.sharding import PartitionSpec as P
 
+MESH = pl.DeviceIdType.MESH
 TOPK = 8
 HEADS = 16
 KVH = 2
+CAP = 10
+GROUPS = 4
+PEERS = 32
+
+
+def my_coords():
+    ctx = lax.axis_index("ctx")
+    exp = lax.axis_index("exp")
+    x = (ctx // 4) * 2 + (exp // 2) % 2
+    return x, ctx % 4, exp // 4, exp % 2
+
+
+def device_at(x, y, z, core):
+    return ((x // 2) * 4 + y, z * 4 + (x % 2) * 2 + core)
+
+
+def offset_parts(o):
+    g, j = o // PEERS, o % PEERS
+    dc, dx, dy = j % 2, (j // 2) % 4, (j // 8) % 4
+    dz = (g + 8 - dx - dy) % 4
+    return dx, dy, dz, dc
+
+
+def peer_to(o):
+    x, y, z, c = my_coords()
+    dx, dy, dz, dc = offset_parts(o)
+    return device_at((x + dx) % 4, (y + dy) % 4, (z + dz) % 4, (c + dc) % 2)
+
+
+def peer_from(o):
+    x, y, z, c = my_coords()
+    dx, dy, dz, dc = offset_parts(o)
+    return device_at((x + 4 - dx) % 4, (y + 4 - dy) % 4, (z + 4 - dz) % 4, (c + 2 - dc) % 2)
+
+
+def offset_of_expert(e):
+    x, y, z, c = my_coords()
+    ce, ee = e // 16, e % 16
+    dx = ((ce // 4) * 2 + (ee // 2) % 2 + 4 - x) % 4
+    dy = (ce % 4 + 4 - y) % 4
+    dz = (ee // 4 + 4 - z) % 4
+    dc = (ee % 2 + 2 - c) % 2
+    return ((dx + dy + dz) % 4) * PEERS + dc + 2 * dx + 8 * dy
+
+
+def moe_kernel(
+    cap,
+    slot_tok, slot_at, shares,
+    x_tiles, resid, w_gate, w_up, w_down,
+    out_ref,
+    send_buf, in_buf, ans_buf, ret_buf, vg, vu, vd, stage, xrows,
+    wsem, dsend, drecv, asend, arecv,
+):
+    copies = [
+        pltpu.make_async_copy(w_gate, vg, wsem.at[0]),
+        pltpu.make_async_copy(w_up, vu, wsem.at[1]),
+        pltpu.make_async_copy(w_down, vd, wsem.at[2]),
+    ]
+    for copy in copies:
+        copy.start()
+    barrier = pltpu.get_barrier_semaphore()
+
+    def greet(o, carry):
+        pl.semaphore_signal(barrier, inc=1, device_id=peer_to(o), device_id_type=MESH)
+        return carry
+
+    lax.fori_loop(1, GROUPS * PEERS, greet, 0)
+    for r in range(cap):
+        in_buf[0, r] = x_tiles[slot_tok[r]]
+
+    def fill(o, carry):
+        for r in range(cap):
+            send_buf[o, r] = x_tiles[slot_tok[o * cap + r]]
+        return carry
+
+    lax.fori_loop(1, PEERS, fill, 0)
+    pl.semaphore_wait(barrier, GROUPS * PEERS - 1)
+
+    def dispatch(o, sem):
+        return pltpu.make_async_remote_copy(
+            src_ref=send_buf.at[o], dst_ref=in_buf.at[o],
+            send_sem=dsend.at[sem], recv_sem=drecv.at[sem],
+            device_id=peer_to(o), device_id_type=MESH,
+        )
+
+    def give_back(o, sem):
+        return pltpu.make_async_remote_copy(
+            src_ref=ans_buf.at[o], dst_ref=ret_buf.at[o],
+            send_sem=asend.at[sem], recv_sem=arecv.at[sem],
+            device_id=peer_from(o), device_id_type=MESH,
+        )
+
+    def send_first(o, carry):
+        dispatch(o, 0).start()
+        return carry
+
+    lax.fori_loop(1, PEERS, send_first, 0)
+
+    def send_rest(o, carry):
+        fill(o, 0)
+        dispatch(o, o // PEERS).start()
+        return carry
+
+    lax.fori_loop(PEERS, GROUPS * PEERS, send_rest, 0)
+    for copy in copies:
+        copy.wait()
+    rows = PEERS * cap
+
+    def compute(g):
+        block = in_buf[pl.ds(g * PEERS, PEERS)]
+        stage[...] = block.astype(jnp.float32).reshape(rows * 16, 128)
+        for s in range(16):
+            xrows[:, s * 128 : (s + 1) * 128] = stage[pl.ds(s, rows, stride=16), :].astype(jnp.bfloat16)
+        rows_in = xrows[...]
+        gate = jnp.dot(rows_in, vg[...], preferred_element_type=jnp.float32)
+        up = jnp.dot(rows_in, vu[...], preferred_element_type=jnp.float32)
+        inner = (gate / (1.0 + jnp.exp(-gate)) * up).astype(jnp.bfloat16)
+        for q in range(4):
+            part = jnp.dot(inner, vd[:, q * 512 : (q + 1) * 512], preferred_element_type=jnp.float32)
+            for s in range(4):
+                stage[pl.ds(q * 4 + s, rows, stride=16), :] = part[:, s * 128 : (s + 1) * 128]
+        return stage[...].astype(jnp.bfloat16).reshape(PEERS, cap, 16, 128)
+
+    def wait_bytes(buf, start, count, sem):
+        pltpu.make_async_copy(buf.at[pl.ds(start, count)], buf.at[pl.ds(start, count)], sem).wait()
+
+    def start_back(o, sem):
+        give_back(o, sem).start()
+        return sem
+
+    for g in range(GROUPS):
+        first = 1 if g == 0 else 0
+        wait_bytes(in_buf, g * PEERS + first, PEERS - first, drecv.at[g])
+        answers = compute(g)
+        if g == 0:
+            ret_buf[0] = answers[0]
+        ans_buf[pl.ds(g * PEERS, PEERS)] = answers
+        lax.fori_loop(g * PEERS + first, (g + 1) * PEERS, lambda o, c, g=g: start_back(o, g), g)
+    for g in range(GROUPS):
+        first = 1 if g == 0 else 0
+        wait_bytes(ret_buf, g * PEERS + first, PEERS - first, arecv.at[g])
+
+    def combine(t, carry):
+        total = jnp.zeros((16, 128), jnp.float32)
+        for k in range(TOPK):
+            at = slot_at[t * TOPK + k]
+            total += shares[t * TOPK + k] * ret_buf[at // cap, at % cap].astype(jnp.float32)
+        out_ref[t] = (resid[t].astype(jnp.float32) + total).astype(jnp.bfloat16)
+        return carry
+
+    lax.fori_loop(0, out_ref.shape[0], combine, 0)
+    for g in range(GROUPS):
+        first = 1 if g == 0 else 0
+        wait_bytes(send_buf, g * PEERS + first, PEERS - first, dsend.at[g])
+        wait_bytes(ans_buf, g * PEERS + first, PEERS - first, asend.at[g])
+
+
+def slots_of(expert_ids, tok_rows, cap):
+    flat = expert_ids.reshape(-1)
+    count = flat.shape[0]
+    ids = jnp.arange(128, dtype=jnp.int32)
+    matches = flat[:, None] == ids[None, :]
+    row = jnp.arange(count, dtype=jnp.int32)
+    earlier = (row[:, None] > row[None, :]).astype(jnp.bfloat16)
+    before = jnp.dot(earlier, matches.astype(jnp.bfloat16), preferred_element_type=jnp.float32)
+    rank = jnp.sum(jnp.where(matches, before, 0.0), axis=1).astype(jnp.int32)
+    slot_at = offset_of_expert(flat) * cap + rank
+    slot_tok = jnp.full((128 * cap,), tok_rows, jnp.int32).at[slot_at].set(row // TOPK)
+    return slot_tok, slot_at
+
+
+def moe(normed_ffn, resid, slot_tok, slot_at, shares, w_gate, w_up, w_down, cap=10):
+    tok, width = normed_ffn.shape
+    ff = w_gate.shape[1]
+    x_tiles = jnp.concatenate([normed_ffn, jnp.zeros((8, width), jnp.bfloat16)], axis=0).reshape(tok + 8, 16, 128)
+    n = GROUPS * PEERS
+    out = pl.pallas_call(
+        functools.partial(moe_kernel, cap),
+        out_shape=jax.ShapeDtypeStruct((tok, 16, 128), jnp.bfloat16),
+        in_specs=[pl.BlockSpec(memory_space=pltpu.SMEM)] * 3
+        + [pl.BlockSpec(memory_space=pltpu.VMEM)] * 2
+        + [pl.BlockSpec(memory_space=pl.ANY)] * 3,
+        out_specs=pl.BlockSpec(memory_space=pltpu.VMEM),
+        scratch_shapes=[pltpu.VMEM((n, cap, 16, 128), jnp.bfloat16)] * 4
+        + [
+            pltpu.VMEM((width, ff), jnp.bfloat16),
+            pltpu.VMEM((width, ff), jnp.bfloat16),
+            pltpu.VMEM((ff, width), jnp.bfloat16),
+            pltpu.VMEM((PEERS * cap * 16, 128), jnp.float32),
+            pltpu.VMEM((PEERS * cap, width), jnp.bfloat16),
+            pltpu.SemaphoreType.DMA((3,)),
+        ]
+        + [pltpu.SemaphoreType.DMA((GROUPS,))] * 4,
+        compiler_params=pltpu.CompilerParams(
+            collective_id=3, has_side_effects=True, vmem_limit_bytes=60 * 1024 * 1024
+        ),
+        name="moe",
+    )(slot_tok, slot_at, shares.reshape(-1), x_tiles, resid.reshape(tok, 16, 128), w_gate, w_up, w_down)
+    return out.reshape(tok, width)
 
 
 epsilon = 1e-06
@@ -160,40 +363,9 @@
     ).astype(jnp.float32)
     resid = (hidden_in.astype(jnp.float32) + projected_out).astype(jnp.bfloat16)
     normed_ffn = rms_scale(resid.astype(jnp.float32), ffn_gain).astype(jnp.bfloat16)
-    local_experts = w_gate.shape[0]
-    device_count = ctx_count * exp_count
-    experts_all = local_experts * device_count
-    capacity = tok_rows * TOPK * 5 // (4 * experts_all)
-    flat_ids = expert_ids.reshape(-1)
-    count_rows = flat_ids.shape[0]
-    matches = flat_ids[:, None] == jnp.arange(experts_all, dtype=jnp.int32)[None, :]
-    row_range = jnp.arange(count_rows, dtype=jnp.int32)
-    earlier = (row_range[:, None] > row_range[None, :]).astype(jnp.bfloat16)
-    before = jnp.dot(earlier, matches.astype(jnp.bfloat16), preferred_element_type=jnp.float32)
-    slot_rank = jnp.sum(jnp.where(matches, before, 0.0), axis=1).astype(jnp.int32)
-    slot_index = flat_ids * capacity + slot_rank
-    slot_table = (
-        jnp.full((experts_all * capacity,), tok_rows, jnp.int32)
-        .at[slot_index]
-        .set(row_range // TOPK)
-    )
-    padded_rows = jnp.concatenate([normed_ffn, jnp.zeros((1, model_width), jnp.bfloat16)], axis=0)
-    outgoing = padded_rows[slot_table].reshape(device_count, local_experts, capacity, model_width)
-    arrived = lax.all_to_all(outgoing, ("ctx", "exp"), split_axis=0, concat_axis=0, tiled=True)
-    rows_in = arrived[:, 0].reshape(-1, model_width)
-    gate_out = jnp.dot(rows_in, w_gate[0], preferred_element_type=jnp.float32)
-    up_out = jnp.dot(rows_in, w_up[0], preferred_element_type=jnp.float32)
-    inner_act = (jax.nn.silu(gate_out) * up_out).astype(jnp.bfloat16)
-    answer = jnp.dot(inner_act, w_down[0], preferred_element_type=jnp.float32).astype(jnp.bfloat16)
-    results = [answer.reshape(arrived.shape[0], arrived.shape[2], model_width)]
-    returned = lax.all_to_all(
-        jnp.stack(results, axis=1), ("ctx", "exp"), split_axis=0, concat_axis=0, tiled=True
-    )
-    flat_back = returned.reshape(experts_all * capacity, model_width)
-    picked = flat_back[slot_index].astype(jnp.float32).reshape(tok_rows, TOPK, model_width)
     shares = gate_weights / jnp.sum(gate_weights, axis=1, keepdims=True)
-    mixture = jnp.sum(shares[:, :, None] * picked, axis=1)
-    return (resid.astype(jnp.float32) + mixture).astype(jnp.bfloat16)
+    slot_tok, slot_at = slots_of(expert_ids, tok_rows, CAP)
+    return moe(normed_ffn, resid, slot_tok, slot_at, shares, w_gate[0], w_up[0], w_down[0], CAP)
 
 
 def solution(mesh):

time: 923 us -> 679 us (0.74)
  Pallas kernels: 0 us -> 167 us
  waiting for transfers between devices: 521 us -> 368 us
  local copies, waits for them, and re-layouts: 151 us -> 36.9 us
  blocking collectives: 105 us -> 0 us
  matrix products: 41.1 us -> 18.3 us
  other arithmetic: 36.3 us -> 25.2 us
    pallas_call x0 -> x1, Pallas kernels: none -> 167 us  [moe(): pl.pallas_call(functools.partial(moe_kernel, cap), out_shape=jax.ShapeDty...]
    all_to_all x1 -> x0, blocking collectives: 105 us -> none  [on_device(): lax.all_to_all(outgoing, ('ctx', 'exp'), split_axis=0, concat_axis=0, til...]
    all_to_all x1 -> x0, waiting for transfers between devices: 102 us -> none  [on_device(): lax.all_to_all(jnp.stack(results, axis=1), ('ctx', 'exp'), split_axis=0,...]
    reduce_scatter x1, waiting for transfers between devices: 230 us -> 175 us  [on_device(): lax.psum_scatter(jnp.dot(attended, w_out, preferred_element_type=jnp.floa...]
    dynamic_slice x16, local copies, waits for them, and re-layouts: 28.5 us -> 2.69 us  [visit_tile(): lax.dynamic_slice_in_dim(key_block, tile_idx * tile_len, tile_len, 0)]
    gather x2 -> x0, local copies, waits for them, and re-layouts: 24 us -> none  [the longest x1 12 us: on_device(): padded_rows[slot_table]]
    dynamic_slice x32, local copies, waits for them, and re-layouts: 41.7 us -> 19.9 us  [visit_tile(): lax.dynamic_slice_in_dim(value_block, tile_idx * tile_len, tile_len, 0)]
    another operation x2 -> x0, local copies, waits for them, and re-layouts: 19.4 us -> none  [the longest x1 9.85 us: on_device(): rows_in = arrived[:, 0].reshape(-1, model_width)]
  transfers between devices with their start and end apart: 5 -> 4, of which waited for: 5 -> 4; matrix products, arithmetic and copies ran while one was open for 2% -> 2% of each run, Pallas kernels for 0% -> 0%
where the time goes in v1:
time: 679 us; the launch traced here: 672 us
  waiting for transfers between devices  368 us (54%)
  Pallas kernels  167 us (25%)
  loops' own time  42.4 us (6%)
  local copies, waits for them, and re-layouts  36.9 us (5%)
  other arithmetic  25.2 us (4%)
  matrix products  18.3 us (3%)
  between operations  13.5 us (2%)
    reduce_scatter x1, waiting for transfers between devices, on_device(): lax.psum_scatter(jnp.dot(attended, w_out, preferred_element_type=jnp.floa...  175 us
    pallas_call x1, Pallas kernels, moe(): pl.pallas_call(functools.partial(moe_kernel, cap), out_shape=jax.ShapeDty...  167 us
    all_gather x1, waiting for transfers between devices, on_device(): value_block = lax.all_gather(value_rows, 'ctx', axis=0, tiled=True)  71.5 us
    all_gather x1, waiting for transfers between devices, on_device(): key_block = lax.all_gather(key_rows, 'ctx', axis=0, tiled=True)  68.9 us
    all_gather x1, waiting for transfers between devices, on_device(): row_piece = lax.all_gather(normed, 'exp', axis=0, tiled=True)  53.4 us
    another operation x1, loops' own time, on_device(): lax.fori_loop(0, piece_len // tile_len, visit_tile, (start_state, start_s...  41.9 us
    dynamic_slice x32, local copies, waits for them, and re-layouts, visit_tile(): lax.dynamic_slice_in_dim(value_block, tile_idx * tile_len, tile_len, 0)  19.9 us
  transfers between devices with their start and end apart: 4, of which 4 were waited for; matrix products, arithmetic and copies ran while one was open for 2% of the time, Pallas kernels for 0%

profile of v1, /device:TPU:0, one launch (start us, length us, event | category | flops | bytes accessed | tf_op | source)
XLA Modules:
  0.0 672.1 jit_solution(5998569984106755236)
XLA Ops:
  6.5 1.3 fusion.62
  7.9 2.0 fusion.64
  10.0 1.3 constant_dynamic-slice_fusion.2
  11.3 53.4 %all-gather.5.cloned.1.call-done = bf16[2048,2048]{1,0:T(8,128)(2,1)} async-done(((bf16[128,2048]{1,0:T(8,128)(2,1)}), bf16[2048,2048]{1,0:T(8,128)(2,1)}) %all-gather.5.cloned.1.call-update) | async-done | bytes 8388624 | tf_op jit(solution)/shard_map/all_gather | solution.py:282
  64.7 5.9 fusion.51
  71.1 2.4 fusion.81
  74.5 2.1 slice.88
  77.9 68.9 %all-gather.9.cloned.1.call-done = bf16[16384,1,128]{0,2,1:T(8,128)(2,1)} async-done(((bf16[2048,1,128]{0,2,1:T(8,128)(2,1)}), bf16[16384,1,128]{0,2,1:T(8,128)(2,1)}) %all-gather.9.cloned.1.call-update) | async-done | bytes 4194320 | tf_op jit(solution)/shard_map/all_gather | solution.py:308
  146.8 71.5 %all-gather.7.cloned.1.call-done = bf16[16384,128]{0,1:T(8,128)(2,1)} async-done(((bf16[2048,128]{0,1:T(8,128)(2,1)}), bf16[16384,128]{0,1:T(8,128)(2,1)}) %all-gather.7.cloned.1.call-update) | async-done | bytes 4194320 | tf_op jit(solution)/shard_map/all_gather | solution.py:309
  218.5 84.7 %while.26 = (s32[]{:T(128)}, f32[1,1024]{1,0:T(1,128)S(1)}, f32[1,1024]{1,0:T(1,128)S(1)}, f32[1024,1,128]{2,0,1:T(8,128)S(1)}, f32[1,1024]{1,0:T(1,128)S(1)}, /...) while((s32[]{:T(128)}, f32[1,1024]{1,0:T(1,128)S(1)}, ...), condition=%wide.region_18.19_spmd, body=%wide.region_8.18_spmd.sunk | while | flops 1103675392 | bytes 31117812 | solution.py:351
  218.5 1.1 constant_dynamic-slice_fusion.5
  221.9 3.1 conditional.5
  223.7 1.3 fusion.29
  226.3 3.1 conditional.4
  228.1 1.3 fusion.11
  229.5 1.1 constant_dynamic-slice_fusion.5
  232.9 3.1 conditional.5
  234.6 1.3 fusion.29
  237.3 1.1 constant_dynamic-slice_fusion.5
  242.0 1.1 constant_dynamic-slice_fusion.5
  246.7 1.1 constant_dynamic-slice_fusion.5
  251.4 1.1 constant_dynamic-slice_fusion.5
  256.2 1.1 constant_dynamic-slice_fusion.5
  260.9 1.1 constant_dynamic-slice_fusion.5
  265.6 1.1 constant_dynamic-slice_fusion.5
  303.7 5.6 convolution_convert_fusion
  312.0 4.9 scatter_custom_fusion.slot_tok
  317.5 174.6 %reduce-scatter.2.cloned.1.call-done = bf16[128,2048]{1,0:T(8,128)(2,1)} async-done(((bf16[2048,2048]{1,0:T(8,128)(2,1)}), bf16[128,2048]{1,0:T(8,128)(2,1)}) %reduce-scatter.2.cloned.1.call-update) | async-done | bytes 524304 | tf_op jit(solution)/shard_map/reduce_scatter | solution.py:358
  492.1 1.3 fusion.59
  493.4 1.3 fusion.151
  496.6 167.0 %moe.1 = bf16[128,16,128]{2,1,0:T(8,128)(2,1)} custom-call(s32[1280]{0:T(1024)} %scatter_custom_fusion.slot_tok, s32[1024]{0:T(1024)} %fusion.123.slot_at, f32[1024]{0:T(1024)} %reshape.866.shares, bf16[136,16,128]{2,1,0:T(8,128)(2,1)} %bitcast.123, bf16[128,16,128]{2,1,0:T(8,128)(2,1)} %bitcast.124, bf16[2048,768]{1,0:T(8,128)(2,1)} %bitcast.120, ...), custom_call_target="tpu_custom_call" | custom-call | tf_op jit(solution)/shard_map/moe/pallas_call | solution.py:191
  663.6 2.0 copy.32
  (161 shorter events, 37.4 us)
Async XLA Ops:
  6.5 297.2 %copy-start = (bf16[128,2048]{1,0:T(8,128)(2,1)S(1)}, bf16[128,2048]{1,0:T(8,128)(2,1)}, u32[]{:S(2)}) copy-start(bf16[128,2048]{1,0:T(8,128)(2,1)} %param.27) | copy-start | bytes 1572868
  6.5 58.2 %copy-start.8 = (bf16[2048,128]{1,0:T(8,128)(2,1)S(1)}, bf16[2048,128]{1,0:T(8,128)(2,1)}, u32[]{:S(2)}) copy-start(bf16[2048,128]{1,0:T(8,128)(2,1)} %param.22) | copy-start | bytes 1572868
  6.5 58.2 %all-gather.5.cloned.1.call-start = ((), (), s32[]{:S(2)}) async-start(), calls=%async_computation.1 | async-start | bytes 8912896 | tf_op jit(solution)/shard_map/all_gather | solution.py:282
  9.9 136.9 %all-gather.9.cloned.1.call-start = ((), (), s32[]{:S(2)}) async-start(), calls=%async_computation.4 | async-start | bytes 4718592 | tf_op jit(solution)/shard_map/all_gather | solution.py:308
  64.7 6.1 copy-start.6
  64.7 6.2 copy-start.7
  70.6 2.9 copy-start.2
  74.4 144.0 %all-gather.7.cloned.1.call-start = ((), (), s32[]{:S(2)}) async-start(), calls=%async_computation.2 | async-start | bytes 4718592 | tf_op jit(solution)/shard_map/all_gather | solution.py:309
  76.6 415.4 %reduce-scatter.2.cloned.1.call-start = ((), (), s32[]{:S(2)}) async-start(), calls=%async_computation.3 | async-start | bytes 8912896 | tf_op jit(solution)/shard_map/reduce_scatter | solution.py:358
  309.3 0.7 copy-start.5
  309.3 1.7 copy-start.3
  309.3 182.8 %copy-start.1 = (bf16[128,2048]{1,0:T(8,128)(2,1)S(1)}, bf16[128,2048]{1,0:T(8,128)(2,1)}, u32[]{:S(2)}) copy-start(bf16[128,2048]{1,0:T(8,128)(2,1)} %param.20) | copy-start | bytes 1572868
  309.3 184.1 %copy-start.4 = (f32[2048]{0:T(1024)S(1)}, f32[2048]{0:T(1024)}, u32[]{:S(2)}) copy-start(f32[2048]{0:T(1024)} %param.28) | copy-start | bytes 24580
Sparse Core Ops, SparseCore 0:
  10.0 54.6 all-gather.4
  74.5 72.2 all-gather.8
  149.2 69.1 all-gather.6
  309.4 182.6 reduce-scatter.1

commit v2 on v1

v2 whole, which is shorter than its diff:
```python
import functools
import math

import jax
import jax.numpy as jnp
from jax import lax
from jax.experimental import pallas as pl
from jax.experimental.pallas import tpu as pltpu
from jax.sharding import PartitionSpec as P

MESH = pl.DeviceIdType.MESH
TOPK = 8
CAP = 10
HEADS = 16
GROUPS = 4
PEERS = 32


def my_coords():
    ctx = lax.axis_index("ctx")
    exp = lax.axis_index("exp")
    x = (ctx // 4) * 2 + (exp // 2) % 2
    return x, ctx % 4, exp // 4, exp % 2


def device_at(x, y, z, core):
    return ((x // 2) * 4 + y, z * 4 + (x % 2) * 2 + core)


def offset_parts(o):
    g, j = o // PEERS, o % PEERS
    dc, dx, dy = j % 2, (j // 2) % 4, (j // 8) % 4
    dz = (g + 8 - dx - dy) % 4
    return dx, dy, dz, dc


def peer_to(o):
    x, y, z, c = my_coords()
    dx, dy, dz, dc = offset_parts(o)
    return device_at((x + dx) % 4, (y + dy) % 4, (z + dz) % 4, (c + dc) % 2)


def peer_from(o):
    x, y, z, c = my_coords()
    dx, dy, dz, dc = offset_parts(o)
    return device_at((x + 4 - dx) % 4, (y + 4 - dy) % 4, (z + 4 - dz) % 4, (c + 2 - dc) % 2)


def offset_of_expert(e):
    x, y, z, c = my_coords()
    ce, ee = e // 16, e % 16
    dx = ((ce // 4) * 2 + (ee // 2) % 2 + 4 - x) % 4
    dy = (ce % 4 + 4 - y) % 4
    dz = (ee // 4 + 4 - z) % 4
    dc = (ee % 2 + 2 - c) % 2
    return ((dx + dy + dz) % 4) * PEERS + dc + 2 * dx + 8 * dy


epsilon = 1e-06
rope_base = 1000000.0


def rms_scale(values, gains):
    return values * lax.rsqrt(jnp.mean(values * values, axis=-1, keepdims=True) + epsilon) * gains


def rope(values, cosine, sine):
    return values * cosine + pltpu.roll(values, 64, 1) * sine


def push(src, dst, ssem, rsem, device):
    pltpu.make_async_remote_copy(
        src_ref=src, dst_ref=dst, send_sem=ssem, recv_sem=rsem,
        device_id=device, device_id_type=MESH,
    ).start()


def wait_for(ref, sem):
    pltpu.make_async_copy(ref, ref, sem).wait()


class Ring:
    def __init__(self, blocks, halves, plus, minus, ssem, rsem, source=None):
        self.own, self.left, self.right = blocks
        self.left_half, self.right_half, self.far_first, self.far_second = halves
        self.plus, self.minus, self.ssem, self.rsem = plus, minus, ssem, rsem
        self.source = self.own if source is None else source

    def start(self):
        push(self.source, self.own, self.ssem.at[0], self.rsem.at[0], self.plus)
        push(self.source, self.own, self.ssem.at[1], self.rsem.at[1], self.minus)

    def forward_left(self):
        wait_for(self.left, self.rsem.at[0])
        push(self.left_half, self.left_half, self.ssem.at[2], self.rsem.at[2], self.plus)

    def forward_right(self):
        wait_for(self.right, self.rsem.at[1])
        push(self.right_half, self.right_half, self.ssem.at[3], self.rsem.at[3], self.minus)

    def finish(self):
        wait_for(self.far_first, self.rsem.at[2])
        wait_for(self.far_second, self.rsem.at[3])

    def drain(self):
        wait_for(self.source, self.ssem.at[0])
        wait_for(self.source, self.ssem.at[1])
        wait_for(self.left_half, self.ssem.at[2])
        wait_for(self.right_half, self.ssem.at[3])


def qkv_kernel(
    hidden, attn_gain, wq, wk, wv, q_gain, k_gain, cosine, sine,
    q_out, kv_out,
    wq_all, normed, kv_stage, q_stage,
    own_sem, wq_s, wq_r, n_s, n_r, z_s, z_r, short_s, short_r, long_s, long_r, d_s, d_r, q_s, q_r,
):
    x, y, z, core = my_coords()
    ctx = lax.axis_index("ctx")
    x_lo = x % 2
    sibling = device_at(x, y, z, 1 - core)
    x_other = (x // 2) * 2 + 1 - x_lo
    x_near = device_at(x_other, y, z, core)
    far_ctx = jnp.where(z < 2, ctx, 7 - ctx)

    def head_device(block, zz):
        return (block, zz * 4 + x_lo * 2 + core)

    own_wq = pltpu.make_async_copy(wq, wq_all.at[z], own_sem)
    own_wq.start()
    barrier = pltpu.get_barrier_semaphore()

    def greet(device):
        pl.semaphore_signal(barrier, inc=1, device_id=device, device_id_type=MESH)

    for dz in range(4):
        for dc in range(2):
            if dz + dc > 0:
                greet(device_at(x, y, (z + dz) % 4, (core + dc) % 2))
        greet(head_device(7 - ctx, dz))
    for d in (1, 3):
        greet(device_at((x + d) % 4, y, z, core))
        greet(device_at(x, (y + d) % 4, z, core))
    mine = x_lo * 2 + core
    normed[mine] = rms_scale(hidden[...].astype(jnp.float32), attn_gain[...]).astype(jnp.bfloat16)
    pl.semaphore_wait(barrier, 15)

    def wq_half(zz, half):
        return wq_all.at[zz, pl.ds(half * 1024, 1024)]

    z_left, z_right, z_far = (z + 3) % 4, (z + 1) % 4, (z + 2) % 4
    wq_ring = Ring(
        (wq_all.at[z], wq_all.at[z_left], wq_all.at[z_right]),
        (wq_half(z_left, 0), wq_half(z_right, 1), wq_half(z_far, 0), wq_half(z_far, 1)),
        device_at(x, y, z_right, core), device_at(x, y, z_left, core), wq_s, wq_r, wq,
    )
    other = (1 - x_lo) * 2 + core
    push(normed.at[mine], normed.at[mine], n_s.at[1], n_r.at[1], x_near)
    push(normed.at[mine], normed.at[mine], n_s.at[0], n_r.at[0], sibling)
    wq_ring.start()

    here = pl.ds(mine * 128, 128)
    own_normed = normed[mine]
    key_raw = jnp.dot(own_normed, wk[...], preferred_element_type=jnp.float32)
    value_raw = jnp.dot(own_normed, wv[...], preferred_element_type=jnp.float32)
    for g in range(2):
        cols = slice(g * 128, (g + 1) * 128)
        key = rope(rms_scale(key_raw[:, cols], k_gain[...]), cosine[here, :], sine[here, :])
        kv_stage[0, g] = key.astype(jnp.bfloat16)
        kv_stage[1, g] = value_raw[:, cols].astype(jnp.bfloat16)

    def piece(which, xx, yy, zz, cc):
        return kv_out.at[which, xx // 2, yy, zz, xx % 2, pl.ds(cc * 128, 128)]

    for which in range(2):
        for zz in range(4):
            is_self = (zz == z) & (which == core)
            src = kv_stage.at[which, zz // 2]
            dst = piece(which, x, y, z, core)

            @pl.when(is_self)
            def _(src=src, dst=dst):
                pltpu.make_async_copy(src, dst, z_r.at[z * 2 + core]).start()

            @pl.when(jnp.logical_not(is_self))
            def _(src=src, dst=dst, which=which, zz=zz):
                push(src, dst, z_s.at[which * 4 + zz], z_r.at[z * 2 + core], device_at(x, y, zz, which))

    for zz in range(4):
        for cc in range(2):
            wait_for(piece(core, x, y, zz, cc), z_r.at[zz * 2 + cc])

    step_x, step_y = 1 - core, core

    def column(n, zs=None):
        xx, yy = (x + n * step_x) % 4, (y + n * step_y) % 4
        if zs is None:
            return kv_out.at[core, xx // 2, yy, :, xx % 2]
        return kv_out.at[core, xx // 2, yy, pl.ds(zs * 2, 2), xx % 2]

    short = Ring(
        (column(0), column(3), column(1)),
        (column(3, 0), column(1, 1), column(2, 0), column(2, 1)),
        device_at((x + step_x) % 4, (y + step_y) % 4, z, core),
        device_at((x + 3 * step_x) % 4, (y + 3 * step_y) % 4, z, core), short_s, short_r,
    )
    short.start()
    short.forward_left()
    short.forward_right()
    short.finish()

    def keys_of(n, half=None):
        yy = (y + n) % 4
        return kv_out.at[0, :, yy] if half is None else kv_out.at[0, half, yy]

    def values_of(n, half=None):
        xx = (x + n) % 4
        if half is None:
            return kv_out.at[1, xx // 2, :, :, xx % 2]
        return kv_out.at[1, xx // 2, pl.ds(half * 2, 2), :, xx % 2]

    def long_ring(of, plus, minus):
        return Ring(
            (of(0), of(3), of(1)), (of(3, 0), of(1, 1), of(2, 0), of(2, 1)), plus, minus, long_s, long_r
        )

    def rings():
        return (
            long_ring(keys_of, device_at(x, (y + 1) % 4, z, core), device_at(x, (y + 3) % 4, z, core)),
            long_ring(values_of, device_at((x + 1) % 4, y, z, core), device_at((x + 3) % 4, y, z, core)),
        )

    both = (keys_of, values_of)

    def on_core(body):
        for index in range(2):
            pl.when(core == index)(lambda index=index: body(index))

    def begin(index):
        rings()[index].start()
        push(both[index](0), both[index](0), d_s.at[0], d_r.at[0], sibling)

    on_core(begin)

    wq_ring.forward_left()
    wq_ring.forward_right()
    wait_for(normed.at[other], n_r.at[1])
    push(normed.at[other], normed.at[other], n_s.at[2], n_r.at[2], sibling)
    wait_for(normed.at[x_lo * 2 + 1 - core], n_r.at[0])
    own_wq.wait()
    wq_ring.finish()
    wait_for(normed.at[(1 - x_lo) * 2 + 1 - core], n_r.at[2])

    tokens = normed[...].reshape(512, 2048)
    for pair in range(2):
        weights = jnp.concatenate([wq_all[2 * pair], wq_all[2 * pair + 1]], axis=1)
        raw = jnp.dot(tokens, weights, preferred_element_type=jnp.float32)
        for k in range(2):
            query = rope(rms_scale(raw[:, k * 128 : (k + 1) * 128], q_gain[...]), cosine[...], sine[...])
            q_stage[2 * pair + k] = query.astype(jnp.bfloat16)

    def q_rows(zz):
        return q_out.at[zz // 2, pl.ds((zz % 2) * 512, 512)]

    for zz in range(4):
        is_self = (zz == z) & (z < 2)

        @pl.when(is_self)
        def _(zz=zz):
            pltpu.make_async_copy(q_stage.at[zz], q_rows(z), q_r.at[z]).start()

        @pl.when(jnp.logical_not(is_self))
        def _(zz=zz):
            push(q_stage.at[zz], q_rows(z), q_s.at[zz], q_r.at[z], head_device(far_ctx, zz))

    def later(index):
        ring, of = rings()[index], both[index]
        ring.forward_left()
        push(of(3), of(3), d_s.at[1], d_r.at[1], sibling)
        ring.forward_right()
        push(of(1), of(1), d_s.at[2], d_r.at[2], sibling)
        ring.finish()
        push(of(2), of(2), d_s.at[3], d_r.at[3], sibling)
        theirs = both[1 - index]
        for k, n in enumerate((0, 3, 1, 2)):
            wait_for(theirs(n), d_r.at[k])
        ring.drain()
        for k, n in enumerate((0, 3, 1, 2)):
            wait_for(of(n), d_s.at[k])

    on_core(later)
    for zz in range(4):
        wait_for(q_rows(zz), q_r.at[zz])
    wq_ring.drain()
    short.drain()
    wait_for(normed.at[mine], n_s.at[0])
    wait_for(normed.at[mine], n_s.at[1])
    wait_for(normed.at[other], n_s.at[2])
    for zz in range(4):

        @pl.when(jnp.logical_not((zz == z) & (z < 2)))
        def _(zz=zz):
            wait_for(q_stage.at[zz], q_s.at[zz])

        for which in range(2):

            @pl.when(jnp.logical_not((zz == z) & (which == core)))
            def _(zz=zz, which=which):
                wait_for(kv_stage.at[which, zz // 2], z_s.at[which * 4 + zz])


def project(hidden, attn_gain, wq, wk, wv, q_gain, k_gain, cosine, sine):
    vmem = pl.BlockSpec(memory_space=pltpu.VMEM)
    anywhere = pl.BlockSpec(memory_space=pl.ANY)
    dma = pltpu.SemaphoreType.DMA
    return pl.pallas_call(
        qkv_kernel,
        out_shape=(
            jax.ShapeDtypeStruct((2, 1024, 128), jnp.bfloat16),
            jax.ShapeDtypeStruct((2, 2, 4, 4, 2, 256, 128), jnp.bfloat16),
        ),
        in_specs=[vmem, vmem, anywhere] + [vmem] * 6,
        out_specs=(anywhere, anywhere),
        scratch_shapes=[
            pltpu.VMEM((4, 2048, 128), jnp.bfloat16),
            pltpu.VMEM((4, 128, 2048), jnp.bfloat16),
            pltpu.VMEM((2, 2, 128, 128), jnp.bfloat16),
            pltpu.VMEM((4, 512, 128), jnp.bfloat16),
            dma, dma((4,)), dma((4,)), dma((3,)), dma((3,)), dma((8,)), dma((8,)),
            dma((4,)), dma((4,)), dma((4,)), dma((4,)), dma((4,)), dma((4,)), dma((4,)), dma((4,)),
        ],
        compiler_params=pltpu.CompilerParams(
            collective_id=1, has_side_effects=True, vmem_limit_bytes=40 * 1024 * 1024
        ),
        name="project",
    )(hidden, attn_gain.reshape(1, -1), wq, wk, wv, q_gain.reshape(1, -1), k_gain.reshape(1, -1), cosine, sine)


QB = 256
TK = 1024


def flash_kernel(q_ref, kv_ref, o_ref, m_scr, acc_scr):
    ctx = lax.axis_index("ctx")
    half_rows = q_ref.shape[1]
    scale = math.log2(math.e) / math.sqrt(128)
    blocks = half_rows // QB

    def step(q, k, v, m_prev, acc, first_row):
        s = lax.dot_general(q, k, (((1,), (1,)), ((), ())), preferred_element_type=jnp.float32)
        if first_row is not None:
            row = lax.broadcasted_iota(jnp.int32, s.shape, 0) + first_row
            col = lax.broadcasted_iota(jnp.int32, s.shape, 1)
            s = jnp.where(col <= row, s, -1e30)
        m_new = jnp.maximum(m_prev, jnp.max(s, axis=1, keepdims=True))
        alpha = jnp.exp2((m_prev - m_new) * scale)
        shift = (m_new * scale)[:, :1]
        p = jnp.exp2(s * scale - shift).astype(jnp.bfloat16)
        joined = jnp.concatenate([v, jnp.ones_like(v)], axis=1)
        pv = jnp.dot(p, joined, preferred_element_type=jnp.float32)
        return m_new, acc * jnp.concatenate([alpha, alpha], axis=1) + pv

    for half in range(2):
        h = 2 * ctx if half == 0 else 15 - 2 * ctx
        m_scr[...] = jnp.full_like(m_scr, -1e30)
        acc_scr[...] = jnp.zeros_like(acc_scr)

        def tile(t, carry, half=half):
            k = kv_ref[0, pl.ds(t * TK, TK), :]
            v = kv_ref[1, pl.ds(t * TK, TK), :]
            for b in range(blocks):
                rows = pl.ds(b * QB, QB)
                m, a = step(q_ref[half, rows, :], k, v, m_scr[rows, :], acc_scr[rows, :], None)
                m_scr[rows, :] = m
                acc_scr[rows, :] = a
            return carry

        lax.fori_loop(0, h * (half_rows // TK), tile, 0)
        base = h * half_rows
        for b in range(blocks):
            rows = pl.ds(b * QB, QB)
            seen = (b + 1) * QB
            k = kv_ref[0, pl.ds(base, seen), :]
            v = kv_ref[1, pl.ds(base, seen), :]
            m, a = step(q_ref[half, rows, :], k, v, m_scr[rows, :], acc_scr[rows, :], b * QB)
            o_ref[half, rows, :] = (a[:, :128] / a[:, 128:]).astype(jnp.bfloat16)


def flash(q, kv):
    vmem = pl.BlockSpec(memory_space=pltpu.VMEM)
    return pl.pallas_call(
        flash_kernel,
        out_shape=jax.ShapeDtypeStruct(q.shape, jnp.bfloat16),
        in_specs=[vmem, vmem],
        out_specs=vmem,
        scratch_shapes=[
            pltpu.VMEM((q.shape[1], 128), jnp.float32),
            pltpu.VMEM((q.shape[1], 256), jnp.float32),
        ],
        compiler_params=pltpu.CompilerParams(vmem_limit_bytes=50 * 1024 * 1024),
        cost_estimate=pl.CostEstimate(flops=9 * 10**9, bytes_accessed=9 * 2**20, transcendentals=17 * 2**20),
        name="flash",
    )(q, kv)


def moe_kernel(
    cap,
    slot_tok, slot_at, shares,
    attended, hidden, ffn_gain, w_out, w_gate, w_up, w_down,
    out_ref,
    send_buf, in_buf, ans_buf, ret_buf, vo, vg, vu, vd, stage, xrows, x_tiles, heads, resid,
    wsem, osend, orecv, dsend, drecv, asend, arecv,
):
    ctx = lax.axis_index("ctx")
    exp = lax.axis_index("exp")
    tok = hidden.shape[0]
    copies = [
        pltpu.make_async_copy(w_gate, vg, wsem.at[0]),
        pltpu.make_async_copy(w_up, vu, wsem.at[1]),
        pltpu.make_async_copy(w_down, vd, wsem.at[2]),
        pltpu.make_async_copy(w_out, vo, wsem.at[3]),
    ]
    for copy in copies:
        copy.start()
    barrier = pltpu.get_barrier_semaphore()

    def greet(o, carry):
        pl.semaphore_signal(barrier, inc=1, device_id=peer_to(o), device_id_type=MESH)
        return carry

    lax.fori_loop(1, GROUPS * PEERS, greet, 0)
    x_tiles[tok:] = jnp.zeros((8, 16, 128), jnp.bfloat16)
    pl.semaphore_wait(barrier, GROUPS * PEERS - 1)
    my_columns = pl.ds(pl.multiple_of(exp * 128, 128), 128)

    def head_rows(e):
        return attended.at[e // 8, pl.ds((e % 8) * 128, 128)]

    def swap(e, carry):
        is_self = (e == exp) & (e < 8)

        @pl.when(is_self)
        def _():
            pltpu.make_async_copy(head_rows(e), heads.at[:, my_columns], orecv).start()

        @pl.when(jnp.logical_not(is_self))
        def _():
            push(
                head_rows(e), heads.at[:, my_columns], osend, orecv,
                (jnp.where(e < 8, ctx, 7 - ctx), e),
            )

        return carry

    lax.fori_loop(0, HEADS, swap, 0)
    copies[3].wait()
    wait_for(heads, orecv)
    projected = jnp.dot(heads[...], vo[...], preferred_element_type=jnp.float32)
    summed = (hidden[...].astype(jnp.float32) + projected).astype(jnp.bfloat16)
    resid[...] = summed
    normed = rms_scale(summed.astype(jnp.float32), ffn_gain[...])
    for s in range(16):
        stage[pl.ds(s, tok, stride=16), :] = normed[:, s * 128 : (s + 1) * 128]
    x_tiles[:tok] = stage[: tok * 16].astype(jnp.bfloat16).reshape(tok, 16, 128)

    for r in range(cap):
        in_buf[0, r] = x_tiles[slot_tok[r]]

    def fill(o, carry):
        for r in range(cap):
            send_buf[o, r] = x_tiles[slot_tok[o * cap + r]]
        return carry


    def dispatch(o, sem):
        return pltpu.make_async_remote_copy(
            src_ref=send_buf.at[o], dst_ref=in_buf.at[o],
            send_sem=dsend.at[sem], recv_sem=drecv.at[sem],
            device_id=peer_to(o), device_id_type=MESH,
        )

    def give_back(o, sem):
        return pltpu.make_async_remote_copy(
            src_ref=ans_buf.at[o], dst_ref=ret_buf.at[o],
            send_sem=asend.at[sem], recv_sem=arecv.at[sem],
            device_id=peer_from(o), device_id_type=MESH,
        )

    def send(o, carry):
        fill(o, 0)
        dispatch(o, o // PEERS).start()
        return carry

    lax.fori_loop(1, GROUPS * PEERS, send, 0)
    for copy in copies[:3]:
        copy.wait()
    rows = PEERS * cap

    def compute(g):
        block = in_buf[pl.ds(g * PEERS, PEERS)]
        stage[...] = block.astype(jnp.float32).reshape(rows * 16, 128)
        for s in range(16):
            xrows[:, s * 128 : (s + 1) * 128] = stage[pl.ds(s, rows, stride=16), :].astype(jnp.bfloat16)
        rows_in = xrows[...]
        gate = jnp.dot(rows_in, vg[...], preferred_element_type=jnp.float32)
        up = jnp.dot(rows_in, vu[...], preferred_element_type=jnp.float32)
        inner = (gate / (1.0 + jnp.exp(-gate)) * up).astype(jnp.bfloat16)
        for q in range(4):
            part = jnp.dot(inner, vd[:, q * 512 : (q + 1) * 512], preferred_element_type=jnp.float32)
            for s in range(4):
                stage[pl.ds(q * 4 + s, rows, stride=16), :] = part[:, s * 128 : (s + 1) * 128]
        return stage[...].astype(jnp.bfloat16).reshape(PEERS, cap, 16, 128)

    def wait_bytes(buf, start, count, sem):
        pltpu.make_async_copy(buf.at[pl.ds(start, count)], buf.at[pl.ds(start, count)], sem).wait()

    def start_back(o, sem):
        give_back(o, sem).start()
        return sem

    for g in range(GROUPS):
        first = 1 if g == 0 else 0
        wait_bytes(in_buf, g * PEERS + first, PEERS - first, drecv.at[g])
        answers = compute(g)
        if g == 0:
            ret_buf[0] = answers[0]
        ans_buf[pl.ds(g * PEERS, PEERS)] = answers
        lax.fori_loop(g * PEERS + first, (g + 1) * PEERS, lambda o, c, g=g: start_back(o, g), g)
    for g in range(GROUPS):
        first = 1 if g == 0 else 0
        wait_bytes(ret_buf, g * PEERS + first, PEERS - first, arecv.at[g])

    def combine(t, carry):
        total = jnp.zeros((16, 128), jnp.float32)
        for k in range(TOPK):
            at = slot_at[t * TOPK + k]
            total += shares[t * TOPK + k] * ret_buf[at // cap, at % cap].astype(jnp.float32)
        stage[pl.ds(t * 16, 16), :] = total
        return carry

    lax.fori_loop(0, tok, combine, 0)
    for s in range(16):
        cols = slice(s * 128, (s + 1) * 128)
        mixture = stage[pl.ds(s, tok, stride=16), :]
        out_ref[:, cols] = (resid[:, cols].astype(jnp.float32) + mixture).astype(jnp.bfloat16)
    for g in range(GROUPS):
        first = 1 if g == 0 else 0
        wait_bytes(send_buf, g * PEERS + first, PEERS - first, dsend.at[g])
        wait_bytes(ans_buf, g * PEERS + first, PEERS - first, asend.at[g])

    @pl.when(exp < 8)
    def _():
        wait_for(heads.at[:, pl.ds(0, 15 * 128)], osend)

    @pl.when(exp >= 8)
    def _():
        wait_for(heads, osend)


def slots_of(expert_ids, tok_rows, cap):
    flat = expert_ids.reshape(-1)
    count = flat.shape[0]
    ids = jnp.arange(128, dtype=jnp.int32)
    matches = flat[:, None] == ids[None, :]
    row = jnp.arange(count, dtype=jnp.int32)
    earlier = (row[:, None] > row[None, :]).astype(jnp.bfloat16)
    before = jnp.dot(earlier, matches.astype(jnp.bfloat16), preferred_element_type=jnp.float32)
    rank = jnp.sum(jnp.where(matches, before, 0.0), axis=1).astype(jnp.int32)
    slot_at = offset_of_expert(flat) * cap + rank
    slot_tok = jnp.full((128 * cap,), tok_rows, jnp.int32).at[slot_at].set(row // TOPK)
    return slot_tok, slot_at


def tail(attended, hidden, ffn_gain, w_out, slot_tok, slot_at, shares, w_gate, w_up, w_down):
    tok, width = hidden.shape
    ff = w_gate.shape[1]
    n = GROUPS * PEERS
    vmem = pl.BlockSpec(memory_space=pltpu.VMEM)
    anywhere = pl.BlockSpec(memory_space=pl.ANY)
    dma = pltpu.SemaphoreType.DMA
    return pl.pallas_call(
        functools.partial(moe_kernel, CAP),
        out_shape=jax.ShapeDtypeStruct((tok, width), jnp.bfloat16),
        in_specs=[pl.BlockSpec(memory_space=pltpu.SMEM)] * 3 + [vmem] * 3 + [anywhere] * 4,
        out_specs=vmem,
        scratch_shapes=[pltpu.VMEM((n, CAP, 16, 128), jnp.bfloat16)] * 4
        + [
            pltpu.VMEM((width, width), jnp.bfloat16),
            pltpu.VMEM((width, ff), jnp.bfloat16),
            pltpu.VMEM((width, ff), jnp.bfloat16),
            pltpu.VMEM((ff, width), jnp.bfloat16),
            pltpu.VMEM((PEERS * CAP * 16, 128), jnp.float32),
            pltpu.VMEM((PEERS * CAP, width), jnp.bfloat16),
            pltpu.VMEM((tok + 8, 16, 128), jnp.bfloat16),
            pltpu.VMEM((tok, width), jnp.bfloat16),
            pltpu.VMEM((tok, width), jnp.bfloat16),
            dma((4,)), dma, dma, dma((GROUPS,)), dma((GROUPS,)), dma((GROUPS,)), dma((GROUPS,)),
        ],
        compiler_params=pltpu.CompilerParams(
            collective_id=3, has_side_effects=True, vmem_limit_bytes=62 * 1024 * 1024
        ),
        name="tail",
    )(slot_tok, slot_at, shares.reshape(-1), attended, hidden, ffn_gain.reshape(1, -1), w_out, w_gate, w_up, w_down)


def on_device(
    hidden_in, attn_gain, w_query, w_key, w_value, q_gain, k_gain, w_out, ffn_gain,
    w_gate, w_up, w_down, expert_ids, gate_weights,
):
    ctx, exp = lax.axis_index("ctx"), lax.axis_index("exp")
    w_out_all = lax.all_gather(w_out, "exp", axis=0, tiled=True)
    places = ctx * 2048 + (exp // 4) * 512 + jnp.arange(512, dtype=jnp.int32)
    frequency = jnp.exp(jnp.arange(64, dtype=jnp.float32) * (-2.0 * math.log(rope_base) / 128))
    angles = places.astype(jnp.float32)[:, None] * frequency[None, :]
    cosine, sine = jnp.cos(angles), jnp.sin(angles)
    q, kv = project(
        hidden_in, attn_gain, w_query, w_key, w_value, q_gain, k_gain,
        jnp.concatenate([cosine, cosine], axis=1), jnp.concatenate([-sine, sine], axis=1),
    )
    shares = gate_weights / jnp.sum(gate_weights, axis=1, keepdims=True)
    slot_tok, slot_at = slots_of(expert_ids, hidden_in.shape[0], CAP)
    attended = flash(q, kv.reshape(2, 16384, 128))
    return tail(
        attended, hidden_in, ffn_gain, w_out_all, slot_tok, slot_at, shares, w_gate[0], w_up[0], w_down[0]
    )


def solution(mesh):
    placed = (
        P(("ctx", "exp"), None),
        P(),
        P(None, "exp"),
        P(),
        P(),
        P(),
        P(),
        P("exp", None),
        P(),
        P(("ctx", "exp"), None, None),
        P(("ctx", "exp"), None, None),
        P(("ctx", "exp"), None, None),
        P(("ctx", "exp"), None),
        P(("ctx", "exp"), None),
    )
    return jax.shard_map(
        on_device, mesh=mesh, in_specs=placed, out_specs=P(("ctx", "exp"), None), check_vma=False
    )
```

time: 679 us -> 347 us (0.51)
  the two profiles are of different devices: /device:TPU:0 before, /device:TPU:27 now
where the time goes in v2:
time: 347 us
  Pallas kernels  315 us (91%)
  local copies, waits for them, and re-layouts  13.6 us (4%)
  between operations  13.6 us (4%)
  other arithmetic  3.47 us (1%)
    pallas_call x1, Pallas kernels, tail(): pl.pallas_call(functools.partial(moe_kernel, CAP), out_shape=jax.ShapeDty...  197 us
    pallas_call x1, Pallas kernels, project(): pl.pallas_call(qkv_kernel, out_shape=(jax.ShapeDtypeStruct((2, 1024, 128)...  80.4 us
    pallas_call x1, Pallas kernels, flash(): pl.pallas_call(flash_kernel, out_shape=jax.ShapeDtypeStruct(q.shape, jnp....  36.9 us
    unnamed x20, local copies, waits for them, and re-layouts  7.77 us
  transfers between devices with their start and end apart: 1, of which 0 were waited for; matrix products, arithmetic and copies ran while one was open for 3% of the time, Pallas kernels for 34%

profile of v2, /device:TPU:27, one launch (start us, length us, event | category | flops | bytes accessed | tf_op | source)
XLA Modules:
  0.0 346.6 jit_solution(17704389755259380150)
XLA Ops:
  6.5 0.0 copy-start.2
  6.6 0.0 all-gather.2.cloned.1.call-start
  6.6 0.7 all-gather.2.cloned.1.call-update
  7.3 0.8 copy.15
  8.2 0.1 eq.29
  8.3 0.1 reshape.561
  8.4 0.6 fusion.2
  9.0 0.7 reduce_sum.19
  9.7 0.7 broadcast_divide_fusion
  10.4 0.1 copy.17
  10.5 0.7 reshape.562.shares
  11.2 0.2 compare_select_fusion
  11.4 4.9 %scatter_custom_fusion.slot_tok = s32[1280]{0:T(1024)} fusion(s32[1024]{0:T(1024)S(1)} %bitcast.19, s32[1024]{0:T(1024)S(1)} %add_select_fusion.13, s32[]{:T(128)} %constant.179.clone.1), kind=kCustom, calls=%fused_computation.133 | custom fusion | bytes 5124 | tf_op jit(solution)/shard_map/scatter | solution.py:570
  16.3 1.0 fusion.4
  17.3 0.2 pad_maximum_fusion
  17.5 0.0 copy-done.5
  17.5 0.0 copy-done.6
  17.5 0.0 copy-done.7
  17.5 0.0 copy-done
  17.6 0.0 copy-done.1
  17.6 0.0 copy-done.2
  17.6 0.0 copy-start.4
  17.6 1.0 copy-done.4
  18.6 80.4 %project.1 = (bf16[2,1024,128]{2,1,0:T(8,128)(2,1)S(1)}, bf16[2,2,4,4,2,256,128]{6,5,4,3,2,1,0:T(8,128)(2,1)S(1)}) custom-call(bf16[128,2048]{1,0:T(8,128)(2,1)S(1)} %copy-done, f32[1,2048]{1,0:T(1,128)S(1)} %bitcast.10, bf16[2048,128]{1,0:T(8,128)(2,1)S(1)} %copy-done.4, bf16[2048,256]{1,0:T(8,128)(2,1)S(1)} %copy-done.1, bf16[2048,256]{1,0:T(8,128)(2,1)S(1)} %copy-done.2, ...), custom_call_target="tpu_custom_call" | custom-call | tf_op jit(solution)/shard_map/project/pallas_call | solution.py:316
  99.1 0.0 copy-start.8
  99.1 3.2 copy-done.8
  102.3 0.6 fusion.29.slot_at
  102.9 36.9 %flash.1.attended = bf16[2,1024,128]{2,1,0:T(8,128)(2,1)S(1)} custom-call(bf16[2,1024,128]{2,1,0:T(8,128)(2,1)S(1)} %get-tuple-element.7.q_ref, bf16[2,16384,128]{2,1,0:T(8,128)(2,1)} %bitcast.13), custom_call_target="tpu_custom_call" | custom-call | flops 8999999488 | bytes 9437184 | tf_op jit(solution)/shard_map/flash/pallas_call | solution.py:391
  139.8 0.0 copy-start.3
  139.9 0.8 copy-done.3
  140.6 197.2 %tail.1 = bf16[128,2048]{1,0:T(8,128)(2,1)} custom-call(s32[1280]{0:T(1024)} %scatter_custom_fusion.slot_tok, s32[1024]{0:T(1024)} %fusion.29.slot_at, f32[1024]{0:T(1024)} %reshape.562.shares, bf16[2,1024,128]{2,1,0:T(8,128)(2,1)} %copy-done.3, bf16[128,2048]{1,0:T(8,128)(2,1)} %hidden.3, f32[1,2048]{1,0:T(1,128)} %bitcast.18, ...), custom_call_target="tpu_custom_call" | custom-call | tf_op jit(solution)/shard_map/tail/pallas_call | solution.py:581
  337.9 1.9 copy.19
  (10 shorter events, 0.0 us)
Async XLA Ops:
  6.5 11.0 %copy-start.5 = (f32[2048]{0:T(1024)S(1)}, f32[2048]{0:T(1024)}, u32[]{:S(2)}) copy-start(f32[2048]{0:T(1024)} %param.15) | copy-start | bytes 24580
  6.5 11.0 %copy-start.6 = (f32[128]{0:T(128)S(1)}, f32[128]{0:T(128)}, u32[]{:S(2)}) copy-start(f32[128]{0:T(128)} %param.19) | copy-start | bytes 1540
  6.5 11.0 %copy-start.7 = (f32[128]{0:T(128)S(1)}, f32[128]{0:T(128)}, u32[]{:S(2)}) copy-start(f32[128]{0:T(128)} %param.20) | copy-start | bytes 1540
  6.5 11.0 %copy-start = (bf16[128,2048]{1,0:T(8,128)(2,1)S(1)}, bf16[128,2048]{1,0:T(8,128)(2,1)}, u32[]{:S(2)}) copy-start(bf16[128,2048]{1,0:T(8,128)(2,1)} %hidden.3) | copy-start | bytes 1572868
  6.5 11.0 %copy-start.1 = (bf16[2048,256]{1,0:T(8,128)(2,1)S(1)}, bf16[2048,256]{1,0:T(8,128)(2,1)}, u32[]{:S(2)}) copy-start(bf16[2048,256]{1,0:T(8,128)(2,1)} %wk.1) | copy-start | bytes 3145732
  6.5 11.0 %copy-start.2 = (bf16[2048,256]{1,0:T(8,128)(2,1)S(1)}, bf16[2048,256]{1,0:T(8,128)(2,1)}, u32[]{:S(2)}) copy-start(bf16[2048,256]{1,0:T(8,128)(2,1)} %wv.1) | copy-start | bytes 3145732
  6.6 134.1 %all-gather.2.cloned.1.call-start = ((), (), s32[]{:S(2)}) async-start(), calls=%async_computation | async-start | bytes 8912896 | tf_op jit(solution)/shard_map/all_gather | solution.py:611
  17.6 1.0 copy-start.4
  99.1 3.2 copy-start.8
  139.8 0.8 copy-start.3
Sparse Core Ops, SparseCore 0:
  9.1 75.5 all-gather.1

commit v3 on v2

--- a/solution.py
+++ b/solution.py
@@ -28,10 +28,8 @@
 
 
 def offset_parts(o):
-    g, j = o // PEERS, o % PEERS
-    dc, dx, dy = j % 2, (j // 2) % 4, (j // 8) % 4
-    dz = (g + 8 - dx - dy) % 4
-    return dx, dy, dz, dc
+    dc, k, dy, dx = o // 64, (o // 16) % 4, (o // 4) % 4, o % 4
+    return dx, dy, (k + 8 - dx - dy) % 4, dc
 
 
 def peer_to(o):
@@ -48,14 +46,11 @@
 
 def offset_of_expert(e):
     x, y, z, c = my_coords()
-    ce, ee = e // 16, e % 16
-    dx = ((ce // 4) * 2 + (ee // 2) % 2 + 4 - x) % 4
-    dy = (ce % 4 + 4 - y) % 4
-    dz = (ee // 4 + 4 - z) % 4
-    dc = (ee % 2 + 2 - c) % 2
-    return ((dx + dy + dz) % 4) * PEERS + dc + 2 * dx + 8 * dy
-
-
+    dx = (((e >> 6) & 1) * 2 + ((e >> 1) & 1) + 4 - x) & 3
+    dy = ((e >> 4) + 4 - y) & 3
+    dz = ((e >> 2) + 4 - z) & 3
+    dc = (e + 2 - c) & 1
+    return dc * 64 + ((dx + dy + dz) & 3) * 16 + dy * 4 + dx
 epsilon = 1e-06
 rope_base = 1000000.0
 
@@ -109,9 +104,41 @@
         wait_for(self.right_half, self.ssem.at[3])
 
 
+def assign_slots(expert_ids, slot_tok, slot_at):
+    sub = lax.broadcasted_iota(jnp.int32, (128, 128), 0)
+    lane = lax.broadcasted_iota(jnp.int32, (128, 128), 1)
+    eye = (sub == lane).astype(jnp.bfloat16)
+    before = (sub < lane).astype(jnp.bfloat16)
+    ones = jnp.ones((128, 128), jnp.bfloat16)
+    ids = expert_ids[...].astype(jnp.float32).astype(jnp.bfloat16)
+    turned = lax.dot_general(ids, eye, (((0,), (0,)), ((), ())), preferred_element_type=jnp.float32)
+    offsets = offset_of_expert(turned.astype(jnp.int32))
+    base = jnp.zeros((128, 128), jnp.float32)
+    named, ranks = [], []
+    for k in range(TOPK):
+        match = (sub == offsets[k : k + 1, :]).astype(jnp.float32)
+        match_low = match.astype(jnp.bfloat16)
+        place = base + jnp.dot(match_low, before, preferred_element_type=jnp.float32)
+        rank = jnp.sum(match * place, axis=0, keepdims=True)
+        base = base + jnp.dot(match_low, ones, preferred_element_type=jnp.float32)
+        named.append(match)
+        ranks.append(rank)
+        slot_at[k : k + 1, :] = offsets[k : k + 1, :] * CAP + rank.astype(jnp.int32)
+    token = (128 - lane[:8]).astype(jnp.float32).astype(jnp.bfloat16)
+    slot_tok[...] = jnp.full(slot_tok.shape, 128, jnp.int32)
+    for r in range(CAP):
+        chosen = jnp.zeros((128, 128), jnp.float32)
+        for k in range(TOPK):
+            chosen = chosen + jnp.where(ranks[k] == r, named[k], 0.0)
+        found = lax.dot_general(
+            token, chosen.astype(jnp.bfloat16), (((1,), (1,)), ((), ())), preferred_element_type=jnp.float32
+        )
+        slot_tok[r : r + 1, :] = 128 - found[0:1].astype(jnp.int32)
+
+
 def qkv_kernel(
-    hidden, attn_gain, wq, wk, wv, q_gain, k_gain, cosine, sine,
-    q_out, kv_out,
+    hidden, attn_gain, wq, wk, wv, q_gain, k_gain, cosine, sine, expert_ids,
+    q_out, kv_out, slot_tok, slot_at,
     wq_all, normed, kv_stage, q_stage,
     own_sem, wq_s, wq_r, n_s, n_r, z_s, z_r, short_s, short_r, long_s, long_r, d_s, d_r, q_s, q_r,
 ):
@@ -241,6 +268,7 @@
         push(both[index](0), both[index](0), d_s.at[0], d_r.at[0], sibling)
 
     on_core(begin)
+    assign_slots(expert_ids, slot_tok, slot_at)
 
     wq_ring.forward_left()
     wq_ring.forward_right()
@@ -309,7 +337,7 @@
                 wait_for(kv_stage.at[which, zz // 2], z_s.at[which * 4 + zz])
 
 
-def project(hidden, attn_gain, wq, wk, wv, q_gain, k_gain, cosine, sine):
+def project(hidden, attn_gain, wq, wk, wv, q_gain, k_gain, cosine, sine, expert_ids):
     vmem = pl.BlockSpec(memory_space=pltpu.VMEM)
     anywhere = pl.BlockSpec(memory_space=pl.ANY)
     dma = pltpu.SemaphoreType.DMA
@@ -318,9 +346,11 @@
         out_shape=(
             jax.ShapeDtypeStruct((2, 1024, 128), jnp.bfloat16),
             jax.ShapeDtypeStruct((2, 2, 4, 4, 2, 256, 128), jnp.bfloat16),
+            jax.ShapeDtypeStruct((16, 128), jnp.int32),
+            jax.ShapeDtypeStruct((TOPK, 128), jnp.int32),
         ),
-        in_specs=[vmem, vmem, anywhere] + [vmem] * 6,
-        out_specs=(anywhere, anywhere),
+        in_specs=[vmem, vmem, anywhere] + [vmem] * 7,
+        out_specs=(anywhere, anywhere, vmem, vmem),
         scratch_shapes=[
             pltpu.VMEM((4, 2048, 128), jnp.bfloat16),
             pltpu.VMEM((4, 128, 2048), jnp.bfloat16),
@@ -333,18 +363,97 @@
             collective_id=1, has_side_effects=True, vmem_limit_bytes=40 * 1024 * 1024
         ),
         name="project",
-    )(hidden, attn_gain.reshape(1, -1), wq, wk, wv, q_gain.reshape(1, -1), k_gain.reshape(1, -1), cosine, sine)
+    )(hidden, attn_gain.reshape(1, -1), wq, wk, wv, q_gain.reshape(1, -1), k_gain.reshape(1, -1), cosine, sine, expert_ids)
 
 
 QB = 256
 TK = 1024
 
 
-def flash_kernel(q_ref, kv_ref, o_ref, m_scr, acc_scr):
+def flash_kernel(q_ref, kv_ref, w_out, o_ref, w_all, kv, m_scr, acc_scr,
+                 kv_sem, own_sem, a_s, a_r, b_s, b_r, x_s, x_r, d_s, d_r):
+    x, y, z, core = my_coords()
     ctx = lax.axis_index("ctx")
     half_rows = q_ref.shape[1]
     scale = math.log2(math.e) / math.sqrt(128)
     blocks = half_rows // QB
+    tiles = kv_ref.shape[1] // TK
+
+    def tile_copy(t):
+        rows = pl.ds(t * TK, TK)
+        return pltpu.make_async_copy(kv_ref.at[:, rows, :], kv.at[:, rows, :], kv_sem.at[t])
+
+    lax.fori_loop(0, tiles, lambda t, c: (tile_copy(t).start(), c)[1], 0)
+
+    x_lo = x % 2
+    sibling = device_at(x, y, z, 1 - core)
+    x_near = device_at((x // 2) * 2 + 1 - x_lo, y, z, core)
+    plus, minus = device_at(x, y, (z + 1) % 4, core), device_at(x, y, (z + 3) % 4, core)
+    barrier = pltpu.get_barrier_semaphore()
+    for device in (sibling, x_near, plus, minus):
+        pl.semaphore_signal(barrier, inc=1, device_id=device, device_id_type=MESH)
+
+    def shard(dz, xl, cc):
+        return w_all.at[(z + dz) % 4, xl, cc]
+
+    def part(dz, xl, half):
+        return w_all.at[(z + dz) % 4, xl, core, pl.ds(half * 64, 64)]
+
+    ring = Ring(
+        (shard(0, x_lo, core), shard(3, x_lo, core), shard(1, x_lo, core)),
+        (part(3, x_lo, 0), part(1, x_lo, 1), part(2, x_lo, 0), part(2, x_lo, 1)),
+        plus, minus, a_s, a_r, w_out,
+    )
+    x_hi_half = 1 - x_lo
+    order = [(0, 0), (3, 0), (1, 0), (2, 0), (0, 1), (3, 1), (1, 1), (2, 1)]
+
+    def share(n, src=None):
+        dz, flip = order[n]
+        xl = x_hi_half if flip else x_lo
+        push(shard(dz, xl, core) if src is None else src, shard(dz, xl, core), d_s.at[n], d_r.at[n], sibling)
+
+    own = pltpu.make_async_copy(w_out, shard(0, x_lo, core), own_sem)
+
+    def stage_0():
+        own.start()
+        ring.start()
+        push(w_out, shard(0, x_lo, core), x_s.at[0], x_r.at[0], x_near)
+        share(0, w_out)
+
+    def stage_1():
+        ring.forward_left()
+        ring.forward_right()
+        share(1)
+        share(2)
+        theirs = shard(0, x_hi_half, core)
+        wait_for(theirs, x_r.at[0])
+        push(theirs, theirs, b_s.at[0], b_r.at[0], plus)
+        push(theirs, theirs, b_s.at[1], b_r.at[1], minus)
+        share(4)
+
+    def stage_2():
+        ring.finish()
+        push(shard(2, x_lo, core), shard(2, x_lo, core), x_s.at[1], x_r.at[1], x_near)
+        share(3)
+
+    def stage_3():
+        wait_for(shard(3, x_hi_half, core), b_r.at[0])
+        share(5)
+        wait_for(shard(1, x_hi_half, core), b_r.at[1])
+        share(6)
+        wait_for(shard(2, x_hi_half, core), x_r.at[1])
+        share(7)
+
+    def stage_4():
+        for n, (dz, flip) in enumerate(order):
+            wait_for(shard(dz, x_hi_half if flip else x_lo, 1 - core), d_r.at[n])
+            wait_for(shard(dz, x_hi_half if flip else x_lo, core), d_s.at[n])
+        own.wait()
+        ring.drain()
+        wait_for(w_out, x_s.at[0])
+        wait_for(w_out, x_s.at[1])
+        wait_for(w_out, b_s.at[0])
+        wait_for(w_out, b_s.at[1])
 
     def step(q, k, v, m_prev, acc, first_row):
         s = lax.dot_general(q, k, (((1,), (1,)), ((), ())), preferred_element_type=jnp.float32)
@@ -360,52 +469,76 @@
         pv = jnp.dot(p, joined, preferred_element_type=jnp.float32)
         return m_new, acc * jnp.concatenate([alpha, alpha], axis=1) + pv
 
+    m_scr[...] = jnp.full_like(m_scr, -1e30)
+    acc_scr[...] = jnp.zeros_like(acc_scr)
+    last = (2 * ctx, 15 - 2 * ctx)
+    pl.semaphore_wait(barrier, 4)
+    stage_0()
+
+    def full(half, t):
+        k = kv[0, pl.ds(t * TK, TK), :]
+        v = kv[1, pl.ds(t * TK, TK), :]
+        for b in range(blocks):
+            rows = pl.ds(b * QB, QB)
+            m, a = step(q_ref[half, rows, :], k, v, m_scr[half, rows, :], acc_scr[half, rows, :], None)
+            m_scr[half, rows, :] = m
+            acc_scr[half, rows, :] = a
+
+    def done_by(t):
+        return jnp.minimum(t, last[0]) + jnp.minimum(t, last[1])
+
+    def tile(t, carry):
+        tile_copy(t).wait()
+        done, earlier = done_by(t), done_by(t - 1)
+        pl.when((done >= 6) & (earlier < 6))(stage_1)
+        pl.when((done >= 11) & (earlier < 11))(stage_2)
+        for half in range(2):
+            pl.when(t < last[half])(functools.partial(full, half, t))
+        return carry
+
+    lax.fori_loop(0, tiles, tile, 0)
+    stage_3()
     for half in range(2):
-        h = 2 * ctx if half == 0 else 15 - 2 * ctx
-        m_scr[...] = jnp.full_like(m_scr, -1e30)
-        acc_scr[...] = jnp.zeros_like(acc_scr)
-
-        def tile(t, carry, half=half):
-            k = kv_ref[0, pl.ds(t * TK, TK), :]
-            v = kv_ref[1, pl.ds(t * TK, TK), :]
-            for b in range(blocks):
-                rows = pl.ds(b * QB, QB)
-                m, a = step(q_ref[half, rows, :], k, v, m_scr[rows, :], acc_scr[rows, :], None)
-                m_scr[rows, :] = m
-                acc_scr[rows, :] = a
-            return carry
-
-        lax.fori_loop(0, h * (half_rows // TK), tile, 0)
-        base = h * half_rows
+        base = last[half] * half_rows
         for b in range(blocks):
             rows = pl.ds(b * QB, QB)
             seen = (b + 1) * QB
-            k = kv_ref[0, pl.ds(base, seen), :]
-            v = kv_ref[1, pl.ds(base, seen), :]
-            m, a = step(q_ref[half, rows, :], k, v, m_scr[rows, :], acc_scr[rows, :], b * QB)
+            k = kv[0, pl.ds(base, seen), :]
+            v = kv[1, pl.ds(base, seen), :]
+            m, a = step(q_ref[half, rows, :], k, v, m_scr[half, rows, :], acc_scr[half, rows, :], b * QB)
             o_ref[half, rows, :] = (a[:, :128] / a[:, 128:]).astype(jnp.bfloat16)
-
-
-def flash(q, kv):
+    stage_4()
+
+
+def flash(q, kv, w_out):
     vmem = pl.BlockSpec(memory_space=pltpu.VMEM)
+    anywhere = pl.BlockSpec(memory_space=pl.ANY)
+    dma = pltpu.SemaphoreType.DMA
     return pl.pallas_call(
         flash_kernel,
-        out_shape=jax.ShapeDtypeStruct(q.shape, jnp.bfloat16),
-        in_specs=[vmem, vmem],
-        out_specs=vmem,
+        out_shape=(
+            jax.ShapeDtypeStruct(q.shape, jnp.bfloat16),
+            jax.ShapeDtypeStruct((4, 2, 2, 128, 2048), jnp.bfloat16),
+        ),
+        in_specs=[vmem, anywhere, anywhere],
+        out_specs=(vmem, anywhere),
         scratch_shapes=[
-            pltpu.VMEM((q.shape[1], 128), jnp.float32),
-            pltpu.VMEM((q.shape[1], 256), jnp.float32),
+            pltpu.VMEM(kv.shape, jnp.bfloat16),
+            pltpu.VMEM((2, q.shape[1], 128), jnp.float32),
+            pltpu.VMEM((2, q.shape[1], 256), jnp.float32),
+            dma((kv.shape[1] // TK,)), dma, dma((4,)), dma((4,)), dma((2,)), dma((2,)), dma((2,)), dma((2,)),
+            dma((8,)), dma((8,)),
         ],
-        compiler_params=pltpu.CompilerParams(vmem_limit_bytes=50 * 1024 * 1024),
-        cost_estimate=pl.CostEstimate(flops=9 * 10**9, bytes_accessed=9 * 2**20, transcendentals=17 * 2**20),
+        compiler_params=pltpu.CompilerParams(
+            collective_id=2, has_side_effects=True, vmem_limit_bytes=50 * 1024 * 1024
+        ),
         name="flash",
-    )(q, kv)
+    )(q, kv, w_out)
 
 
 def moe_kernel(
     cap,
-    slot_tok, slot_at, shares,
+    slot_tok, slot_at, gates,
     attended, hidden, ffn_gain, w_out, w_gate, w_up, w_down,
     out_ref,
     send_buf, in_buf, ans_buf, ret_buf, vo, vg, vu, vd, stage, xrows, x_tiles, heads, resid,
@@ -464,11 +597,11 @@
     x_tiles[:tok] = stage[: tok * 16].astype(jnp.bfloat16).reshape(tok, 16, 128)
 
     for r in range(cap):
-        in_buf[0, r] = x_tiles[slot_tok[r]]
+        in_buf[0, r] = x_tiles[slot_tok[r, 0]]
 
     def fill(o, carry):
         for r in range(cap):
-            send_buf[o, r] = x_tiles[slot_tok[o * cap + r]]
+            send_buf[o, r] = x_tiles[slot_tok[r, o]]
         return carry
 
 
@@ -532,9 +665,13 @@
 
     def combine(t, carry):
         total = jnp.zeros((16, 128), jnp.float32)
+        weight = jnp.zeros((16, 128), jnp.float32)
         for k in range(TOPK):
-            at = slot_at[t * TOPK + k]
-            total += shares[t * TOPK + k] * ret_buf[at // cap, at % cap].astype(jnp.float32)
+            at = slot_at[k, t]
+            gate = jnp.full((16, 128), gates[t, k], jnp.float32)
+            weight += gate
+            total += gate * ret_buf[at // cap, at % cap].astype(jnp.float32)
+        total = total / weight
         stage[pl.ds(t * 16, 16), :] = total
         return carry
 
@@ -557,21 +694,7 @@
         wait_for(heads, osend)
 
 
-def slots_of(expert_ids, tok_rows, cap):
-    flat = expert_ids.reshape(-1)
-    count = flat.shape[0]
-    ids = jnp.arange(128, dtype=jnp.int32)
-    matches = flat[:, None] == ids[None, :]
-    row = jnp.arange(count, dtype=jnp.int32)
-    earlier = (row[:, None] > row[None, :]).astype(jnp.bfloat16)
-    before = jnp.dot(earlier, matches.astype(jnp.bfloat16), preferred_element_type=jnp.float32)
-    rank = jnp.sum(jnp.where(matches, before, 0.0), axis=1).astype(jnp.int32)
-    slot_at = offset_of_expert(flat) * cap + rank
-    slot_tok = jnp.full((128 * cap,), tok_rows, jnp.int32).at[slot_at].set(row // TOPK)
-    return slot_tok, slot_at
-
-
-def tail(attended, hidden, ffn_gain, w_out, slot_tok, slot_at, shares, w_gate, w_up, w_down):
+def tail(attended, hidden, ffn_gain, w_out, slot_tok, slot_at, gates, w_gate, w_up, w_down):
     tok, width = hidden.shape
     ff = w_gate.shape[1]
     n = GROUPS * PEERS
@@ -600,7 +723,7 @@
             collective_id=3, has_side_effects=True, vmem_limit_bytes=62 * 1024 * 1024
         ),
         name="tail",
-    )(slot_tok, slot_at, shares.reshape(-1), attended, hidden, ffn_gain.reshape(1, -1), w_out, w_gate, w_up, w_down)
+    )(slot_tok, slot_at, gates, attended, hidden, ffn_gain.reshape(1, -1), w_out, w_gate, w_up, w_down)
 
 
 def on_device(
@@ -608,20 +731,18 @@
     w_gate, w_up, w_down, expert_ids, gate_weights,
 ):
     ctx, exp = lax.axis_index("ctx"), lax.axis_index("exp")
-    w_out_all = lax.all_gather(w_out, "exp", axis=0, tiled=True)
     places = ctx * 2048 + (exp // 4) * 512 + jnp.arange(512, dtype=jnp.int32)
     frequency = jnp.exp(jnp.arange(64, dtype=jnp.float32) * (-2.0 * math.log(rope_base) / 128))
     angles = places.astype(jnp.float32)[:, None] * frequency[None, :]
     cosine, sine = jnp.cos(angles), jnp.sin(angles)
-    q, kv = project(
+    q, kv, slot_tok, slot_at = project(
         hidden_in, attn_gain, w_query, w_key, w_value, q_gain, k_gain,
-        jnp.concatenate([cosine, cosine], axis=1), jnp.concatenate([-sine, sine], axis=1),
+        jnp.concatenate([cosine, cosine], axis=1), jnp.concatenate([-sine, sine], axis=1), expert_ids,
     )
-    shares = gate_weights / jnp.sum(gate_weights, axis=1, keepdims=True)
-    slot_tok, slot_at = slots_of(expert_ids, hidden_in.shape[0], CAP)
-    attended = flash(q, kv.reshape(2, 16384, 128))
+    attended, w_out_all = flash(q, kv.reshape(2, 16384, 128), w_out)
     return tail(
-        attended, hidden_in, ffn_gain, w_out_all, slot_tok, slot_at, shares, w_gate[0], w_up[0], w_down[0]
+        attended, hidden_in, ffn_gain, w_out_all.reshape(2048, 2048), slot_tok, slot_at, gate_weights,
+        w_gate[0], w_up[0], w_down[0],
     )
 
 

time: 347 us -> 290 us (0.84)
  the two profiles are of different devices: /device:TPU:27 before, /device:TPU:0 now
where the time goes in v3:
time: 290 us; the launch traced here: 288 us
  Pallas kernels  273 us (94%)
  local copies, waits for them, and re-layouts  14 us (5%)
    pallas_call x1, Pallas kernels, tail(): pl.pallas_call(functools.partial(moe_kernel, CAP), out_shape=jax.ShapeDty...  163 us
    pallas_call x1, Pallas kernels, project(): pl.pallas_call(qkv_kernel, out_shape=(jax.ShapeDtypeStruct((2, 1024, 128)...  58.2 us
    pallas_call x1, Pallas kernels, flash(): pl.pallas_call(flash_kernel, out_shape=(jax.ShapeDtypeStruct(q.shape, jnp...  51.4 us
    unnamed x29, local copies, waits for them, and re-layouts  14 us

profile of v3, /device:TPU:0, one launch (start us, length us, event | category | flops | bytes accessed | tf_op | source)
XLA Modules:
  0.0 288.1 jit_solution(2997050991873497506)
XLA Ops:
  0.0 0.0 copy-start.4
  0.0 1.0 fusion
  1.0 0.2 pad_maximum_fusion
  1.2 0.8 copy.15.expert_ids
  2.0 0.0 copy-start.1
  2.0 1.0 copy-done.1
  3.1 0.0 copy-start.2
  3.1 1.2 copy-done.2
  4.3 0.0 copy-start.3
  4.3 1.2 copy-done.3
  5.5 0.0 copy-start.6
  5.5 1.0 copy-done.6
  6.6 0.0 copy-start.7
  6.6 0.7 copy-done.7
  7.3 0.0 copy-start.10
  7.3 0.7 copy-done.10
  7.9 0.0 copy-start.11
  7.9 0.7 copy-done.11
  8.6 58.2 %project.1 = (bf16[2,1024,128]{2,1,0:T(8,128)(2,1)S(1)}, bf16[2,2,4,4,2,256,128]{6,5,4,3,2,1,0:T(8,128)(2,1)S(1)}, s32[16,128]{1,0:T(8,128)S(1)}, s32[8,128]{1,0:T(8,128)S(1)}) custom-call(bf16[128,2048]{1,0:T(8,128)(2,1)S(1)} %copy-done.1, f32[1,2048]{1,0:T(1,128)S(1)} %bitcast.10, bf16[2048,128]{1,0:T(8,128)(2,1)S(1)} %copy-done.6, ...), custom_call_target="tpu_custom_call" | custom-call | tf_op jit(solution)/shard_map/project/pallas_call | solution.py:344
  66.7 0.0 copy-start
  66.7 3.2 %copy-done = bf16[2,2,4,4,2,256,128]{6,5,4,3,2,1,0:T(8,128)(2,1)} copy-done((bf16[2,2,4,4,2,256,128]{6,5,4,3,2,1,0:T(8,128)(2,1)}, bf16[2,2,4,4,2,256,128]{6,5,4,3,2,1,0:T(8,128)(2,1)S(1)}, u32[]{:S(2)}) %copy-start) | copy-done | bytes 8388632
  70.0 0.0 copy-start.8
  70.0 0.0 copy-done.4
  70.0 51.4 %flash.1 = (bf16[2,1024,128]{2,1,0:T(8,128)(2,1)S(1)}, bf16[4,2,2,128,2048]{4,3,2,1,0:T(8,128)(2,1)}) custom-call(bf16[2,1024,128]{2,1,0:T(8,128)(2,1)S(1)} %get-tuple-element.13.q_ref, bf16[2,16384,128]{2,1,0:T(8,128)(2,1)} %bitcast.9, bf16[128,2048]{1,0:T(8,128)(2,1)S(1)} %copy-done.4), custom_call_target="tpu_custom_call" | custom-call | tf_op jit(solution)/shard_map/flash/pallas_call | solution.py:517
  121.4 0.0 copy-done.8
  121.4 0.0 copy-done.9
  121.4 0.0 copy-start.5
  121.5 0.8 copy-done.5
  122.2 0.0 copy-done.12
  122.2 0.7 copy.16.gates
  123.0 163.2 %tail.1 = bf16[128,2048]{1,0:T(8,128)(2,1)} custom-call(s32[16,128]{1,0:T(8,128)} %copy-done.8, s32[8,128]{1,0:T(8,128)} %copy-done.9, f32[128,8]{1,0:T(8,128)} %copy.16.gates, bf16[2,1024,128]{2,1,0:T(8,128)(2,1)} %copy-done.5, bf16[128,2048]{1,0:T(8,128)(2,1)} %hidden.3, f32[1,2048]{1,0:T(1,128)} %bitcast.17, bf16[2048,2048]{1,0:T(8,128)(2,1)} %bitcast.13, ...), custom_call_target="tpu_custom_call" | custom-call | tf_op jit(solution)/shard_map/tail/pallas_call | solution.py:704
  286.2 1.9 copy.18
  (4 shorter events, 0.0 us)
Async XLA Ops:
  0.0 70.0 %copy-start.4 = (bf16[128,2048]{1,0:T(8,128)(2,1)S(1)}, bf16[128,2048]{1,0:T(8,128)(2,1)}, u32[]{:S(2)}) copy-start(bf16[128,2048]{1,0:T(8,128)(2,1)} %w_out.1) | copy-start | bytes 1572868
  2.0 1.0 copy-start.1
  3.1 1.2 copy-start.2
  4.3 1.2 copy-start.3
  5.5 1.0 copy-start.6
  6.6 0.7 copy-start.7
  7.3 0.7 copy-start.10
  7.9 0.7 copy-start.11
  66.7 3.2 %copy-start = (bf16[2,2,4,4,2,256,128]{6,5,4,3,2,1,0:T(8,128)(2,1)}, bf16[2,2,4,4,2,256,128]{6,5,4,3,2,1,0:T(8,128)(2,1)S(1)}, u32[]{:S(2)}) copy-start(bf16[2,2,4,4,2,256,128]{6,5,4,3,2,1,0:T(8,128)(2,1)S(1)} %get-tuple-element.14) | copy-start | bytes 25165828
  70.0 51.4 %copy-start.8 = (s32[16,128]{1,0:T(8,128)}, s32[16,128]{1,0:T(8,128)S(1)}, u32[]{:S(2)}) copy-start(s32[16,128]{1,0:T(8,128)S(1)} %get-tuple-element.11.slot_tok) | copy-start | bytes 24580
  70.0 51.5 %copy-start.9 = (s32[8,128]{1,0:T(8,128)}, s32[8,128]{1,0:T(8,128)S(1)}, u32[]{:S(2)}) copy-start(s32[8,128]{1,0:T(8,128)S(1)} %get-tuple-element.12.slot_at) | copy-start | bytes 12292
  70.0 52.3 %copy-start.12 = (f32[128,8]{0,1:T(8,128)S(1)}, f32[128,8]{0,1:T(8,128)}, u32[]{:S(2)}) copy-start(f32[128,8]{0,1:T(8,128)} %param.27) | copy-start | bytes 12292
  121.4 0.8 copy-start.5

commit v4 on v3

v4 whole, which is shorter than its diff:
```python
import functools
import math

import jax
import jax.numpy as jnp
from jax import lax
from jax.experimental import pallas as pl
from jax.experimental.pallas import tpu as pltpu
from jax.sharding import PartitionSpec as P

MESH = pl.DeviceIdType.MESH
TOPK = 8
CAP = 10
GROUPS = 4
PEERS = 32


def my_coords():
    ctx = lax.axis_index("ctx")
    exp = lax.axis_index("exp")
    x = (ctx // 4) * 2 + (exp // 2) % 2
    return x, ctx % 4, exp // 4, exp % 2


def device_at(x, y, z, core):
    return ((x // 2) * 4 + y, z * 4 + (x % 2) * 2 + core)


def offset_parts(o):
    dc, k, dy, dx = o // 64, (o // 16) % 4, (o // 4) % 4, o % 4
    return dx, dy, (k + 8 - dx - dy) % 4, dc


def peer_to(o):
    x, y, z, c = my_coords()
    dx, dy, dz, dc = offset_parts(o)
    return device_at((x + dx) % 4, (y + dy) % 4, (z + dz) % 4, (c + dc) % 2)


def peer_from(o):
    x, y, z, c = my_coords()
    dx, dy, dz, dc = offset_parts(o)
    return device_at((x + 4 - dx) % 4, (y + 4 - dy) % 4, (z + 4 - dz) % 4, (c + 2 - dc) % 2)


def offset_of_expert(e):
    x, y, z, c = my_coords()
    dx = (((e >> 6) & 1) * 2 + ((e >> 1) & 1) + 4 - x) & 3
    dy = ((e >> 4) + 4 - y) & 3
    dz = ((e >> 2) + 4 - z) & 3
    dc = (e + 2 - c) & 1
    return dc * 64 + ((dx + dy + dz) & 3) * 16 + dy * 4 + dx
epsilon = 1e-06
rope_base = 1000000.0


def rms_scale(values, gains):
    return values * lax.rsqrt(jnp.mean(values * values, axis=-1, keepdims=True) + epsilon) * gains


def rope(values, cosine, sine):
    return values * cosine + pltpu.roll(values, 64, 1) * sine


def push(src, dst, ssem, rsem, device):
    pltpu.make_async_remote_copy(
        src_ref=src, dst_ref=dst, send_sem=ssem, recv_sem=rsem,
        device_id=device, device_id_type=MESH,
    ).start()


def wait_for(ref, sem):
    pltpu.make_async_copy(ref, ref, sem).wait()


class Ring:
    def __init__(self, blocks, halves, plus, minus, ssem, rsem, source=None):
        self.own, self.left, self.right = blocks
        self.left_half, self.right_half, self.far_first, self.far_second = halves
        self.plus, self.minus, self.ssem, self.rsem = plus, minus, ssem, rsem
        self.source = self.own if source is None else source

    def start(self):
        push(self.source, self.own, self.ssem.at[0], self.rsem.at[0], self.plus)
        push(self.source, self.own, self.ssem.at[1], self.rsem.at[1], self.minus)

    def forward_left(self):
        wait_for(self.left, self.rsem.at[0])
        push(self.left_half, self.left_half, self.ssem.at[2], self.rsem.at[2], self.plus)

    def forward_right(self):
        wait_for(self.right, self.rsem.at[1])
        push(self.right_half, self.right_half, self.ssem.at[3], self.rsem.at[3], self.minus)

    def finish(self):
        wait_for(self.far_first, self.rsem.at[2])
        wait_for(self.far_second, self.rsem.at[3])

    def drain(self):
        wait_for(self.source, self.ssem.at[0])
        wait_for(self.source, self.ssem.at[1])
        wait_for(self.left_half, self.ssem.at[2])
        wait_for(self.right_half, self.ssem.at[3])


def assign_slots(expert_ids, slot_tok, slot_at):
    sub = lax.broadcasted_iota(jnp.int32, (128, 128), 0)
    lane = lax.broadcasted_iota(jnp.int32, (128, 128), 1)
    before = (sub < lane).astype(jnp.bfloat16)
    ones = jnp.ones((128, 128), jnp.bfloat16)
    offsets = offset_of_expert(expert_ids[...])
    base = jnp.zeros((128, 128), jnp.float32)
    named, ranks = [], []
    for k in range(TOPK):
        match = (sub == offsets[k : k + 1, :]).astype(jnp.float32)
        match_low = match.astype(jnp.bfloat16)
        place = base + jnp.dot(match_low, before, preferred_element_type=jnp.float32)
        rank = jnp.sum(match * place, axis=0, keepdims=True)
        base = base + jnp.dot(match_low, ones, preferred_element_type=jnp.float32)
        named.append(match)
        ranks.append(rank)
    slots = offsets * CAP + jnp.concatenate(ranks, axis=0).astype(jnp.int32)
    slot_at[...] = slots.T
    token = (128 - lane[:8]).astype(jnp.float32).astype(jnp.bfloat16)
    slot_tok[...] = jnp.full(slot_tok.shape, 128, jnp.int32)
    for r in range(CAP):
        chosen = jnp.zeros((128, 128), jnp.float32)
        for k in range(TOPK):
            chosen = chosen + jnp.where(ranks[k] == r, named[k], 0.0)
        found = lax.dot_general(
            token, chosen.astype(jnp.bfloat16), (((1,), (1,)), ((), ())), preferred_element_type=jnp.float32
        )
        slot_tok[r : r + 1, :] = 128 - found[0:1].astype(jnp.int32)


QB = 128
DB = 256
TK = 1024


def attend_kernel(
    hidden_in, attn_gain_in, wq, wk_in, wv_in, q_gain_in, k_gain_in, cosine_in, sine_in, ids_in, w_out,
    heads, w_all, slot_tok, slot_at,
    hidden, attn_gain, wk, wv, q_gain, k_gain, cosine, sine, expert_ids,
    kv, wq_all, normed, kv_stage, q_stage, q_ref, o_ref, m_scr, acc_scr,
    in_sem, own_sem, wq_s, wq_r, n_s, n_r, z_s, z_r, short_s, short_r, long_s, long_r, d_s, d_r, q_s, q_r,
    w_own, a_s, a_r, b_s, b_r, x_s, x_r, w_s, w_r, h_s, h_r,
):
    x, y, z, core = my_coords()
    ctx, exp = lax.axis_index("ctx"), lax.axis_index("exp")
    x_lo = x % 2
    sibling = device_at(x, y, z, 1 - core)
    x_other = (x // 2) * 2 + 1 - x_lo
    x_near = device_at(x_other, y, z, core)
    far_ctx = jnp.where(z < 2, ctx, 7 - ctx)

    loads = [
        pltpu.make_async_copy(src, dst, in_sem.at[i])
        for i, (src, dst) in enumerate(
            [
                (hidden_in, hidden), (attn_gain_in, attn_gain), (wk_in, wk), (wv_in, wv),
                (q_gain_in, q_gain), (k_gain_in, k_gain), (cosine_in, cosine), (sine_in, sine),
                (ids_in, expert_ids),
            ]
        )
    ]
    for load in loads:
        load.start()
    own_wq = pltpu.make_async_copy(wq, wq_all.at[z], own_sem)
    own_wq.start()
    barrier = pltpu.get_barrier_semaphore()

    def greet(device):
        pl.semaphore_signal(barrier, inc=1, device_id=device, device_id_type=MESH)

    def greet_block(e, carry):
        greet((7 - ctx, e))
        pl.when(e != exp)(lambda: greet((ctx, e)))
        return carry

    lax.fori_loop(0, 16, greet_block, 0)
    for d in (1, 3):
        greet(device_at((x + d) % 4, y, z, core))
        greet(device_at(x, (y + d) % 4, z, core))
    mine = x_lo * 2 + core
    loads[0].wait()
    loads[1].wait()
    normed[mine] = rms_scale(hidden[...].astype(jnp.float32), attn_gain[...]).astype(jnp.bfloat16)
    pl.semaphore_wait(barrier, 35)

    def wq_half(zz, half):
        return wq_all.at[zz, pl.ds(half * 1024, 1024)]

    z_left, z_right, z_far = (z + 3) % 4, (z + 1) % 4, (z + 2) % 4
    z_plus, z_minus = device_at(x, y, z_right, core), device_at(x, y, z_left, core)
    wq_ring = Ring(
        (wq_all.at[z], wq_all.at[z_left], wq_all.at[z_right]),
        (wq_half(z_left, 0), wq_half(z_right, 1), wq_half(z_far, 0), wq_half(z_far, 1)),
        z_plus, z_minus, wq_s, wq_r, wq,
    )
    other = (1 - x_lo) * 2 + core
    push(normed.at[mine], normed.at[mine], n_s.at[1], n_r.at[1], x_near)
    push(normed.at[mine], normed.at[mine], n_s.at[0], n_r.at[0], sibling)
    wq_ring.start()

    for load in loads[2:]:
        load.wait()
    here = pl.ds(pl.multiple_of(mine * 128, 128), 128)
    own_normed = normed[mine]
    key_raw = jnp.dot(own_normed, wk[...], preferred_element_type=jnp.float32)
    value_raw = jnp.dot(own_normed, wv[...], preferred_element_type=jnp.float32)
    for g in range(2):
        cols = slice(g * 128, (g + 1) * 128)
        key = rope(rms_scale(key_raw[:, cols], k_gain[...]), cosine[here, :], sine[here, :])
        kv_stage[0, g] = key.astype(jnp.bfloat16)
        kv_stage[1, g] = value_raw[:, cols].astype(jnp.bfloat16)

    def piece(which, zz, cc):
        return kv.at[which, x // 2, y, zz, x_lo, pl.ds(cc * 128, 128)]

    for which in range(2):
        for zz in range(4):
            is_self = (zz == z) & (which == core)
            src = kv_stage.at[which, zz // 2]
            dst = piece(which, z, core)

            @pl.when(is_self)
            def _(src=src, dst=dst):
                pltpu.make_async_copy(src, dst, z_r.at[z * 2 + core]).start()

            @pl.when(jnp.logical_not(is_self))
            def _(src=src, dst=dst, which=which, zz=zz):
                push(src, dst, z_s.at[which * 4 + zz], z_r.at[z * 2 + core], device_at(x, y, zz, which))

    for zz in range(4):
        for cc in range(2):
            wait_for(piece(core, zz, cc), z_r.at[zz * 2 + cc])

    def column(n, zs=None):
        xx = (x + n) % 4
        if zs is None:
            return kv.at[core, xx // 2, y, :, xx % 2]
        return kv.at[core, xx // 2, y, pl.ds(zs * 2, 2), xx % 2]

    short = Ring(
        (column(0), column(3), column(1)),
        (column(3, 0), column(1, 1), column(2, 0), column(2, 1)),
        device_at((x + 1) % 4, y, z, core), device_at((x + 3) % 4, y, z, core), short_s, short_r,
    )
    short.start()
    short.forward_left()
    short.forward_right()
    short.finish()

    def blocks_of(n, which, half=None):
        yy = (y + n) % 4
        return kv.at[which, :, yy] if half is None else kv.at[which, half, yy]

    def mine_of(n, half=None):
        return blocks_of(n, core, half)

    long = Ring(
        (mine_of(0), mine_of(3), mine_of(1)),
        (mine_of(3, 0), mine_of(1, 1), mine_of(2, 0), mine_of(2, 1)),
        device_at(x, (y + 1) % 4, z, core), device_at(x, (y + 3) % 4, z, core), long_s, long_r,
    )

    def share_kv(k, n):
        push(mine_of(n), mine_of(n), d_s.at[k], d_r.at[k], sibling)

    def theirs_kv(k, n):
        wait_for(blocks_of(n, 1 - core), d_r.at[k])

    long.start()
    share_kv(0, 0)
    wq_ring.forward_left()
    wq_ring.forward_right()
    wait_for(normed.at[other], n_r.at[1])
    push(normed.at[other], normed.at[other], n_s.at[2], n_r.at[2], sibling)
    assign_slots(expert_ids, slot_tok, slot_at)
    wait_for(normed.at[x_lo * 2 + 1 - core], n_r.at[0])
    own_wq.wait()
    wq_ring.finish()
    wait_for(normed.at[(1 - x_lo) * 2 + 1 - core], n_r.at[2])

    def q_rows(zz):
        return q_ref.at[zz // 2, pl.ds((zz % 2) * 512, 512)]

    tokens = normed[...].reshape(512, 2048)
    for pair in range(2):
        weights = jnp.concatenate([wq_all[2 * pair], wq_all[2 * pair + 1]], axis=1)
        raw = jnp.dot(tokens, weights, preferred_element_type=jnp.float32)
        for k in range(2):
            zz = 2 * pair + k
            query = rope(rms_scale(raw[:, k * 128 : (k + 1) * 128], q_gain[...]), cosine[...], sine[...])
            q_stage[zz] = query.astype(jnp.bfloat16)
            is_self = (zz == z) & (z < 2)

            @pl.when(is_self)
            def _(zz=zz):
                pltpu.make_async_copy(q_stage.at[zz], q_rows(z), q_r.at[z]).start()

            @pl.when(jnp.logical_not(is_self))
            def _(zz=zz):
                push(q_stage.at[zz], q_rows(z), q_s.at[zz], q_r.at[z], (far_ctx, zz * 4 + x_lo * 2 + core))

    def shard(dz, xl, cc):
        return w_all.at[(z + dz) % 4, xl, cc]

    def part(dz, xl, half):
        return w_all.at[(z + dz) % 4, xl, core, pl.ds(half * 64, 64)]

    ring = Ring(
        (shard(0, x_lo, core), shard(3, x_lo, core), shard(1, x_lo, core)),
        (part(3, x_lo, 0), part(1, x_lo, 1), part(2, x_lo, 0), part(2, x_lo, 1)),
        z_plus, z_minus, a_s, a_r, w_out,
    )
    order = [(0, 0), (3, 0), (1, 0), (2, 0), (0, 1), (3, 1), (1, 1), (2, 1)]

    def share(n, src=None):
        dz, flip = order[n]
        xl = 1 - x_lo if flip else x_lo
        push(shard(dz, xl, core) if src is None else src, shard(dz, xl, core), w_s.at[n], w_r.at[n], sibling)

    own = pltpu.make_async_copy(w_out, shard(0, x_lo, core), w_own)
    own.start()
    ring.start()
    push(w_out, shard(0, x_lo, core), x_s.at[0], x_r.at[0], x_near)
    share(0, w_out)

    def stage_1():
        long.forward_left()
        long.forward_right()
        share_kv(1, 3)
        share_kv(2, 1)
        ring.forward_left()
        ring.forward_right()
        share(1)
        share(2)
        theirs = shard(0, 1 - x_lo, core)
        wait_for(theirs, x_r.at[0])
        push(theirs, theirs, b_s.at[0], b_r.at[0], z_plus)
        push(theirs, theirs, b_s.at[1], b_r.at[1], z_minus)
        share(4)
        theirs_kv(1, 3)

    def stage_2():
        ring.finish()
        push(shard(2, x_lo, core), shard(2, x_lo, core), x_s.at[1], x_r.at[1], x_near)
        share(3)
        theirs_kv(2, 1)

    def stage_3():
        long.finish()
        share_kv(3, 2)
        theirs_kv(3, 2)

    def stage_4():
        wait_for(shard(3, 1 - x_lo, core), b_r.at[0])
        share(5)
        wait_for(shard(1, 1 - x_lo, core), b_r.at[1])
        share(6)
        wait_for(shard(2, 1 - x_lo, core), x_r.at[1])
        share(7)

    scale = math.log2(math.e) / math.sqrt(128)

    def step(q, k, v, m_prev, acc, first_row):
        s = lax.dot_general(q, k, (((1,), (1,)), ((), ())), preferred_element_type=jnp.float32)
        if first_row is not None:
            row = lax.broadcasted_iota(jnp.int32, s.shape, 0) + first_row
            col = lax.broadcasted_iota(jnp.int32, s.shape, 1)
            s = jnp.where(col <= row, s, -1e30)
        m_new = jnp.maximum(m_prev, jnp.max(s, axis=1, keepdims=True))
        alpha = jnp.exp2((m_prev - m_new) * scale)
        shift = (m_new * scale)[:, :1]
        p = jnp.exp2(s * scale - shift).astype(jnp.bfloat16)
        joined = jnp.concatenate([v, jnp.ones_like(v)], axis=1)
        pv = jnp.dot(p, joined, preferred_element_type=jnp.float32)
        return m_new, acc * jnp.concatenate([alpha, alpha], axis=1) + pv

    m_scr[...] = jnp.full_like(m_scr, -1e30)
    acc_scr[...] = jnp.zeros_like(acc_scr)
    last = (2 * ctx, 15 - 2 * ctx)

    def tile_of(t):
        at = (t // 8, (t // 2) % 4, pl.ds((t % 2) * 2, 2))
        return kv[(0, *at)].reshape(TK, 128), kv[(1, *at)].reshape(TK, 128)

    def full(half, t):
        k, v = tile_of(t)
        for b in range(1024 // QB):
            rows = pl.ds(b * QB, QB)
            m, a = step(q_ref[half, rows, :], k, v, m_scr[half, rows, :], acc_scr[half, rows, :], None)
            m_scr[half, rows, :] = m
            acc_scr[half, rows, :] = a

    for zz in range(4):
        wait_for(q_rows(zz), q_r.at[zz])
    theirs_kv(0, 0)

    def visit(s, carry):
        pl.when(s == 1)(stage_1)
        pl.when(s == 2)(stage_2)
        pl.when(s == 3)(stage_3)
        n = jnp.where(s == 1, 3, jnp.where(s == 2, 1, jnp.where(s == 3, 2, 0)))
        yy = (y + n) % 4

        def one(u, carry):
            t = ((u // 4) * 4 + yy) * 2 + (u // 2) % 2
            half = u % 2
            pl.when(t < jnp.where(half == 0, last[0], last[1]))(functools.partial(full, half, t))
            return carry

        return lax.fori_loop(0, 8, one, carry)

    lax.fori_loop(0, 4, visit, 0)
    stage_4()
    my_columns = pl.ds(pl.multiple_of(exp * 128, 128), 128)
    for half in range(2):
        k, v = tile_of(last[half])
        for b in range(1024 // DB):
            rows = pl.ds(b * DB, DB)
            seen = (b + 1) * DB
            m, a = step(
                q_ref[half, rows, :], k[:seen], v[:seen], m_scr[half, rows, :], acc_scr[half, rows, :], b * DB
            )
            o_ref[half, rows, :] = (a[:, :128] / a[:, 128:]).astype(jnp.bfloat16)
            for i in range(2):
                e = half * 8 + b * 2 + i
                src = o_ref.at[half, pl.ds(b * DB + i * 128, 128)]
                dst = heads.at[:, my_columns]
                if half:
                    push(src, dst, h_s, h_r, (7 - ctx, e))
                else:
                    pl.when(e == exp)(lambda src=src: pltpu.make_async_copy(src, dst, h_r).start())
                    pl.when(e != exp)(lambda src=src, e=e: push(src, dst, h_s, h_r, (ctx, e)))

    for n, (dz, flip) in enumerate(order):
        wait_for(shard(dz, 1 - x_lo if flip else x_lo, 1 - core), w_r.at[n])
        wait_for(shard(dz, 1 - x_lo if flip else x_lo, core), w_s.at[n])
    own.wait()
    ring.drain()
    for sem in (x_s.at[0], x_s.at[1], b_s.at[0], b_s.at[1]):
        wait_for(w_out, sem)
    long.drain()
    for k, n in enumerate((0, 3, 1, 2)):
        wait_for(mine_of(n), d_s.at[k])
    wq_ring.drain()
    short.drain()
    wait_for(normed.at[mine], n_s.at[0])
    wait_for(normed.at[mine], n_s.at[1])
    wait_for(normed.at[other], n_s.at[2])
    for zz in range(4):

        @pl.when(jnp.logical_not((zz == z) & (z < 2)))
        def _(zz=zz):
            wait_for(q_stage.at[zz], q_s.at[zz])

        for which in range(2):

            @pl.when(jnp.logical_not((zz == z) & (which == core)))
            def _(zz=zz, which=which):
                wait_for(kv_stage.at[which, zz // 2], z_s.at[which * 4 + zz])

    wait_for(heads, h_r)

    @pl.when(exp < 8)
    def _():
        wait_for(heads.at[:, pl.ds(0, 15 * 128)], h_s)

    @pl.when(exp >= 8)
    def _():
        wait_for(heads, h_s)


def attend(hidden, attn_gain, wq, wk, wv, q_gain, k_gain, cosine, sine, ids, w_out):
    vmem = pl.BlockSpec(memory_space=pltpu.VMEM)
    anywhere = pl.BlockSpec(memory_space=pl.ANY)
    dma = pltpu.SemaphoreType.DMA
    low, f32 = jnp.bfloat16, jnp.float32
    return pl.pallas_call(
        attend_kernel,
        out_shape=(
            jax.ShapeDtypeStruct((128, 2048), low),
            jax.ShapeDtypeStruct((4, 2, 2, 128, 2048), low),
            jax.ShapeDtypeStruct((16, 128), jnp.int32),
            jax.ShapeDtypeStruct((128, TOPK), jnp.int32),
        ),
        in_specs=[anywhere] * 11,
        out_specs=(anywhere, anywhere, vmem, vmem),
        scratch_shapes=[
            pltpu.VMEM((128, 2048), low),
            pltpu.VMEM((1, 2048), f32),
            pltpu.VMEM((2048, 256), low),
            pltpu.VMEM((2048, 256), low),
            pltpu.VMEM((1, 128), f32),
            pltpu.VMEM((1, 128), f32),
            pltpu.VMEM((512, 128), f32),
            pltpu.VMEM((512, 128), f32),
            pltpu.VMEM((TOPK, 128), jnp.int32),
            pltpu.VMEM((2, 2, 4, 4, 2, 256, 128), low),
            pltpu.VMEM((4, 2048, 128), low),
            pltpu.VMEM((4, 128, 2048), low),
            pltpu.VMEM((2, 2, 128, 128), low),
            pltpu.VMEM((4, 512, 128), low),
            pltpu.VMEM((2, 1024, 128), low),
            pltpu.VMEM((2, 1024, 128), low),
            pltpu.VMEM((2, 1024, 128), f32),
            pltpu.VMEM((2, 1024, 256), f32),
            dma((9,)), dma, dma((4,)), dma((4,)), dma((3,)), dma((3,)), dma((8,)), dma((8,)),
            dma((4,)), dma((4,)), dma((4,)), dma((4,)), dma((4,)), dma((4,)), dma((4,)), dma((4,)),
            dma, dma((4,)), dma((4,)), dma((2,)), dma((2,)), dma((2,)), dma((2,)), dma((8,)), dma((8,)), dma, dma,
        ],
        compiler_params=pltpu.CompilerParams(
            collective_id=1, has_side_effects=True, vmem_limit_bytes=60 * 1024 * 1024
        ),
        name="attend",
    )(
        hidden, attn_gain.reshape(1, -1), wq, wk, wv, q_gain.reshape(1, -1), k_gain.reshape(1, -1),
        cosine, sine, ids, w_out,
    )


def moe_kernel(
    cap,
    slot_tok,
    heads_in, hidden_in, ffn_gain_in, slot_in, gates_in, w_out, w_gate, w_up, w_down,
    out_ref,
    send_buf, in_buf, ans_buf, ret_buf, vo, vg, vu, vd, stage, xrows, x_tiles, resid, acc,
    heads, hidden, ffn_gain, slot_at, gates,
    wsem, insem, dsend, drecv, asend, arecv,
):
    tok = hidden.shape[0]
    loads = [
        pltpu.make_async_copy(src, dst, insem.at[i])
        for i, (src, dst) in enumerate(
            [(heads_in, heads), (w_out, vo), (hidden_in, hidden), (ffn_gain_in, ffn_gain),
             (slot_in, slot_at), (gates_in, gates)]
        )
    ]
    for load in loads:
        load.start()
    copies = [
        pltpu.make_async_copy(w_gate, vg, wsem.at[0]),
        pltpu.make_async_copy(w_up, vu, wsem.at[1]),
        pltpu.make_async_copy(w_down, vd, wsem.at[2]),
    ]
    for copy in copies:
        copy.start()
    barrier = pltpu.get_barrier_semaphore()

    def greet(o, carry):
        pl.semaphore_signal(barrier, inc=1, device_id=peer_to(o), device_id_type=MESH)
        return carry

    lax.fori_loop(1, GROUPS * PEERS, greet, 0)
    x_tiles[tok:] = jnp.zeros((8, 16, 128), jnp.bfloat16)
    for load in loads:
        load.wait()
    projected = jnp.dot(heads[...], vo[...], preferred_element_type=jnp.float32)
    summed = (hidden[...].astype(jnp.float32) + projected).astype(jnp.bfloat16)
    resid[...] = summed
    normed = rms_scale(summed.astype(jnp.float32), ffn_gain[...])
    for s in range(16):
        stage[pl.ds(s, tok, stride=16), :] = normed[:, s * 128 : (s + 1) * 128]
    x_tiles[:tok] = stage[: tok * 16].astype(jnp.bfloat16).reshape(tok, 16, 128)

    for r in range(cap):
        in_buf[0, r] = x_tiles[slot_tok[r, 0]]
    pl.semaphore_wait(barrier, GROUPS * PEERS - 1)

    def fill(o, carry):
        for r in range(cap):
            send_buf[o, r] = x_tiles[slot_tok[r, o]]
        return carry


    def dispatch(o, sem):
        return pltpu.make_async_remote_copy(
            src_ref=send_buf.at[o], dst_ref=in_buf.at[o],
            send_sem=dsend.at[sem], recv_sem=drecv.at[sem],
            device_id=peer_to(o), device_id_type=MESH,
        )

    def give_back(o, sem):
        return pltpu.make_async_remote_copy(
            src_ref=ans_buf.at[o], dst_ref=ret_buf.at[o],
            send_sem=asend.at[sem], recv_sem=arecv.at[sem],
            device_id=peer_from(o), device_id_type=MESH,
        )

    def send(o, carry):
        fill(o, 0)
        dispatch(o, o // PEERS).start()
        return carry

    lax.fori_loop(1, GROUPS * PEERS, send, 0)
    for copy in copies[:3]:
        copy.wait()
    rows = PEERS * cap

    def rows_of(buf, g):
        block = buf[pl.ds(g * PEERS, PEERS)]
        stage[...] = block.astype(jnp.float32).reshape(rows * 16, 128)
        for s in range(16):
            xrows[:, s * 128 : (s + 1) * 128] = stage[pl.ds(s, rows, stride=16), :].astype(jnp.bfloat16)
        return xrows[...]

    def compute(g):
        rows_in = rows_of(in_buf, g)
        gate = jnp.dot(rows_in, vg[...], preferred_element_type=jnp.float32)
        up = jnp.dot(rows_in, vu[...], preferred_element_type=jnp.float32)
        inner = (gate / (1.0 + jnp.exp(-gate)) * up).astype(jnp.bfloat16)
        for q in range(4):
            part = jnp.dot(inner, vd[:, q * 512 : (q + 1) * 512], preferred_element_type=jnp.float32)
            for s in range(4):
                stage[pl.ds(q * 4 + s, rows, stride=16), :] = part[:, s * 128 : (s + 1) * 128]
        return stage[...].astype(jnp.bfloat16).reshape(PEERS, cap, 16, 128)

    def wait_bytes(buf, start, count, sem):
        pltpu.make_async_copy(buf.at[pl.ds(start, count)], buf.at[pl.ds(start, count)], sem).wait()

    def start_back(o, sem):
        give_back(o, sem).start()
        return sem

    for g in range(GROUPS):
        first = 1 if g == 0 else 0
        wait_bytes(in_buf, g * PEERS + first, PEERS - first, drecv.at[g])
        answers = compute(g)
        if g == 0:
            ret_buf[0] = answers[0]
        ans_buf[pl.ds(g * PEERS, PEERS)] = answers
        lax.fori_loop(g * PEERS + first, (g + 1) * PEERS, lambda o, c, g=g: start_back(o, g), g)
    acc[...] = resid[...].astype(jnp.float32)
    weights = gates[...]
    shares = weights / jnp.sum(weights, axis=1, keepdims=True)
    at = slot_at[...]
    for g in range(GROUPS):
        slot = lax.broadcasted_iota(jnp.int32, (tok, rows), 1) + g * rows
        mix = jnp.zeros((tok, rows), jnp.float32)
        for k in range(TOPK):
            mix = mix + jnp.where(at[:, k : k + 1] == slot, shares[:, k : k + 1], 0.0)
        high = mix.astype(jnp.bfloat16)
        low = (mix - high.astype(jnp.float32)).astype(jnp.bfloat16)
        first = 1 if g == 0 else 0
        wait_bytes(ret_buf, g * PEERS + first, PEERS - first, arecv.at[g])
        back = rows_of(ret_buf, g)
        acc[...] += jnp.dot(high, back, preferred_element_type=jnp.float32) + jnp.dot(
            low, back, preferred_element_type=jnp.float32
        )
    out_ref[...] = acc[...].astype(jnp.bfloat16)
    for g in range(GROUPS):
        first = 1 if g == 0 else 0
        wait_bytes(send_buf, g * PEERS + first, PEERS - first, dsend.at[g])
        wait_bytes(ans_buf, g * PEERS + first, PEERS - first, asend.at[g])


def tail(heads, hidden, ffn_gain, w_out, slot_tok, slot_at, gates, w_gate, w_up, w_down):
    tok, width = hidden.shape
    ff = w_gate.shape[1]
    n = GROUPS * PEERS
    anywhere = pl.BlockSpec(memory_space=pl.ANY)
    dma = pltpu.SemaphoreType.DMA
    low, f32 = jnp.bfloat16, jnp.float32
    return pl.pallas_call(
        functools.partial(moe_kernel, CAP),
        out_shape=jax.ShapeDtypeStruct((tok, width), low),
        in_specs=[pl.BlockSpec(memory_space=pltpu.SMEM)] + [anywhere] * 9,
        out_specs=pl.BlockSpec(memory_space=pltpu.VMEM),
        scratch_shapes=[pltpu.VMEM((n, CAP, 16, 128), low)] * 4
        + [
            pltpu.VMEM((width, width), low),
            pltpu.VMEM((width, ff), low),
            pltpu.VMEM((width, ff), low),
            pltpu.VMEM((ff, width), low),
            pltpu.VMEM((PEERS * CAP * 16, 128), f32),
            pltpu.VMEM((PEERS * CAP, width), low),
            pltpu.VMEM((tok + 8, 16, 128), low),
            pltpu.VMEM((tok, width), low),
            pltpu.VMEM((tok, width), f32),
            pltpu.VMEM((tok, width), low),
            pltpu.VMEM((tok, width), low),
            pltpu.VMEM((1, width), f32),
            pltpu.VMEM((tok, TOPK), jnp.int32),
            pltpu.VMEM((tok, TOPK), f32),
            dma((3,)), dma((6,)), dma((GROUPS,)), dma((GROUPS,)), dma((GROUPS,)), dma((GROUPS,)),
        ],
        compiler_params=pltpu.CompilerParams(
            collective_id=3, has_side_effects=True, vmem_limit_bytes=62 * 1024 * 1024
        ),
        name="tail",
    )(slot_tok, heads, hidden, ffn_gain.reshape(1, -1), slot_at, gates, w_out, w_gate, w_up, w_down)


def on_device(
    hidden_in, attn_gain, w_query, w_key, w_value, q_gain, k_gain, w_out, ffn_gain,
    w_gate, w_up, w_down, expert_ids, gate_weights,
):
    ctx, exp = lax.axis_index("ctx"), lax.axis_index("exp")
    places = ctx * 2048 + (exp // 4) * 512 + jnp.arange(512, dtype=jnp.int32)
    frequency = jnp.exp(jnp.arange(64, dtype=jnp.float32) * (-2.0 * math.log(rope_base) / 128))
    angles = places.astype(jnp.float32)[:, None] * frequency[None, :]
    cosine, sine = jnp.cos(angles), jnp.sin(angles)
    heads, w_out_all, slot_tok, slot_at = attend(
        hidden_in, attn_gain, w_query, w_key, w_value, q_gain, k_gain,
        jnp.concatenate([cosine, cosine], axis=1), jnp.concatenate([-sine, sine], axis=1), expert_ids.T, w_out,
    )
    return tail(
        heads, hidden_in, ffn_gain, w_out_all.reshape(2048, 2048), slot_tok, slot_at, gate_weights,
        w_gate[0], w_up[0], w_down[0],
    )


def solution(mesh):
    placed = (
        P(("ctx", "exp"), None),
        P(),
        P(None, "exp"),
        P(),
        P(),
        P(),
        P(),
        P("exp", None),
        P(),
        P(("ctx", "exp"), None, None),
        P(("ctx", "exp"), None, None),
        P(("ctx", "exp"), None, None),
        P(("ctx", "exp"), None),
        P(("ctx", "exp"), None),
    )
    return jax.shard_map(
        on_device, mesh=mesh, in_specs=placed, out_specs=P(("ctx", "exp"), None), check_vma=False
    )
```

time: 290 us -> 265 us (0.914)
  Pallas kernels: 273 us -> 259 us
  local copies, waits for them, and re-layouts: 14 us -> 2.62 us
    pallas_call x1, Pallas kernels: 163 us -> 150 us  [tail(): pl.pallas_call(functools.partial(moe_kernel, CAP), out_shape=jax.ShapeDty...]
    unnamed x29 -> x4, local copies, waits for them, and re-layouts: 14 us -> 2.62 us
    pallas_call x2 -> x1, Pallas kernels: 110 us -> 109 us  [attend(): pl.pallas_call(attend_kernel, out_shape=(jax.ShapeDtypeStruct((128, 2048)...]
where the time goes in v4:
time: 265 us; the launch traced here: 264 us
  Pallas kernels  259 us (98%)
    pallas_call x1, Pallas kernels, tail(): pl.pallas_call(functools.partial(moe_kernel, CAP), out_shape=jax.ShapeDty...  150 us
    pallas_call x1, Pallas kernels, attend(): pl.pallas_call(attend_kernel, out_shape=(jax.ShapeDtypeStruct((128, 2048)...  109 us

profile of v4, /device:TPU:0, one launch (start us, length us, event | category | flops | bytes accessed | tf_op | source)
XLA Modules:
  0.0 263.6 jit_solution(13722461914279756706)
XLA Ops:
  0.0 0.0 copy-start
  0.0 1.0 fusion
  1.0 1.0 pad_maximum_fusion
  2.0 108.7 %attend.1 = (bf16[128,2048]{1,0:T(8,128)(2,1)}, bf16[4,2,2,128,2048]{4,3,2,1,0:T(8,128)(2,1)}, s32[16,128]{1,0:T(8,128)}, s32[128,8]{1,0:T(8,128)}) custom-call(bf16[128,2048]{1,0:T(8,128)(2,1)} %hidden_in.3, f32[1,2048]{1,0:T(1,128)} %bitcast.13, bf16[2048,128]{1,0:T(8,128)(2,1)} %wq.1, bf16[2048,256]{1,0:T(8,128)(2,1)} %wk_in.1, bf16[2048,256]{1,0:T(8,128)(2,1)} %wv_in.1, ...), custom_call_target="tpu_custom_call" | custom-call | tf_op jit(solution)/shard_map/attend/pallas_call | solution.py:482
  110.7 0.0 copy-done
  110.7 0.7 copy.15.gates_in
  111.4 150.3 %tail.1 = bf16[128,2048]{1,0:T(8,128)(2,1)} custom-call(s32[16,128]{1,0:T(8,128)} %get-tuple-element.9.slot_tok, bf16[128,2048]{1,0:T(8,128)(2,1)} %get-tuple-element.10.heads_in, bf16[128,2048]{1,0:T(8,128)(2,1)} %hidden_in.3, f32[1,2048]{1,0:T(1,128)} %bitcast.14, s32[128,8]{1,0:T(8,128)} %get-tuple-element.11.slot_in, f32[128,8]{1,0:T(8,128)} %copy.15.gates_in, ...), custom_call_target="tpu_custom_call" | custom-call | tf_op jit(solution)/shard_map/tail/pallas_call | solution.py:667
  261.7 1.9 copy.17
  (2 shorter events, 0.0 us)
Async XLA Ops:
  0.0 110.7 %copy-start = (f32[128,8]{0,1:T(8,128)S(1)}, f32[128,8]{0,1:T(8,128)}, u32[]{:S(2)}) copy-start(f32[128,8]{0,1:T(8,128)} %param.27) | copy-start | bytes 12292

commit v5 on v4

--- a/solution.py
+++ b/solution.py
@@ -74,33 +74,35 @@
 
 
 class Ring:
-    def __init__(self, blocks, halves, plus, minus, ssem, rsem, source=None):
+    def __init__(self, blocks, halves, plus, minus, ssem, rsem, source=None, base=0):
         self.own, self.left, self.right = blocks
         self.left_half, self.right_half, self.far_first, self.far_second = halves
-        self.plus, self.minus, self.ssem, self.rsem = plus, minus, ssem, rsem
+        self.plus, self.minus = plus, minus
+        self.ssem = [ssem.at[base + i] for i in range(4)]
+        self.rsem = [rsem.at[base + i] for i in range(4)]
         self.source = self.own if source is None else source
 
     def start(self):
-        push(self.source, self.own, self.ssem.at[0], self.rsem.at[0], self.plus)
-        push(self.source, self.own, self.ssem.at[1], self.rsem.at[1], self.minus)
+        push(self.source, self.own, self.ssem[0], self.rsem[0], self.plus)
+        push(self.source, self.own, self.ssem[1], self.rsem[1], self.minus)
 
     def forward_left(self):
-        wait_for(self.left, self.rsem.at[0])
-        push(self.left_half, self.left_half, self.ssem.at[2], self.rsem.at[2], self.plus)
+        wait_for(self.left, self.rsem[0])
+        push(self.left_half, self.left_half, self.ssem[2], self.rsem[2], self.plus)
 
     def forward_right(self):
-        wait_for(self.right, self.rsem.at[1])
-        push(self.right_half, self.right_half, self.ssem.at[3], self.rsem.at[3], self.minus)
+        wait_for(self.right, self.rsem[1])
+        push(self.right_half, self.right_half, self.ssem[3], self.rsem[3], self.minus)
 
     def finish(self):
-        wait_for(self.far_first, self.rsem.at[2])
-        wait_for(self.far_second, self.rsem.at[3])
+        wait_for(self.far_first, self.rsem[2])
+        wait_for(self.far_second, self.rsem[3])
 
     def drain(self):
-        wait_for(self.source, self.ssem.at[0])
-        wait_for(self.source, self.ssem.at[1])
-        wait_for(self.left_half, self.ssem.at[2])
-        wait_for(self.right_half, self.ssem.at[3])
+        wait_for(self.source, self.ssem[0])
+        wait_for(self.source, self.ssem[1])
+        wait_for(self.left_half, self.ssem[2])
+        wait_for(self.right_half, self.ssem[3])
 
 
 def assign_slots(expert_ids, slot_tok, slot_at):
@@ -152,7 +154,6 @@
     sibling = device_at(x, y, z, 1 - core)
     x_other = (x // 2) * 2 + 1 - x_lo
     x_near = device_at(x_other, y, z, core)
-    far_ctx = jnp.where(z < 2, ctx, 7 - ctx)
 
     loads = [
         pltpu.make_async_copy(src, dst, in_sem.at[i])
@@ -201,7 +202,6 @@
     other = (1 - x_lo) * 2 + core
     push(normed.at[mine], normed.at[mine], n_s.at[1], n_r.at[1], x_near)
     push(normed.at[mine], normed.at[mine], n_s.at[0], n_r.at[0], sibling)
-    wq_ring.start()
 
     for load in loads[2:]:
         load.wait()
@@ -232,6 +232,7 @@
             def _(src=src, dst=dst, which=which, zz=zz):
                 push(src, dst, z_s.at[which * 4 + zz], z_r.at[z * 2 + core], device_at(x, y, zz, which))
 
+    wq_ring.start()
     for zz in range(4):
         for cc in range(2):
             wait_for(piece(core, zz, cc), z_r.at[zz * 2 + cc])
@@ -247,10 +248,33 @@
         (column(3, 0), column(1, 1), column(2, 0), column(2, 1)),
         device_at((x + 1) % 4, y, z, core), device_at((x + 3) % 4, y, z, core), short_s, short_r,
     )
+    def column_ring(n):
+        xx = (x + n) % 4
+
+        def at(dy, half=None):
+            yy = (y + dy) % 4
+            if half is None:
+                return kv.at[core, xx // 2, yy, :, xx % 2]
+            return kv.at[core, xx // 2, yy, pl.ds(half * 2, 2), xx % 2]
+
+        return Ring(
+            (at(0), at(3), at(1)), (at(3, 0), at(1, 1), at(2, 0), at(2, 1)),
+            device_at(x, (y + 1) % 4, z, core), device_at(x, (y + 3) % 4, z, core), long_s, long_r, None, 4 * n,
+        )
+
+    columns = [column_ring(n) for n in range(4)]
     short.start()
+    columns[0].start()
     short.forward_left()
+    columns[3].start()
     short.forward_right()
+    columns[1].start()
+    wq_ring.forward_left()
+    wq_ring.forward_right()
     short.finish()
+    columns[2].start()
+    columns[0].forward_left()
+    columns[0].forward_right()
 
     def blocks_of(n, which, half=None):
         yy = (y + n) % 4
@@ -259,50 +283,50 @@
     def mine_of(n, half=None):
         return blocks_of(n, core, half)
 
-    long = Ring(
-        (mine_of(0), mine_of(3), mine_of(1)),
-        (mine_of(3, 0), mine_of(1, 1), mine_of(2, 0), mine_of(2, 1)),
-        device_at(x, (y + 1) % 4, z, core), device_at(x, (y + 3) % 4, z, core), long_s, long_r,
-    )
-
     def share_kv(k, n):
         push(mine_of(n), mine_of(n), d_s.at[k], d_r.at[k], sibling)
 
     def theirs_kv(k, n):
         wait_for(blocks_of(n, 1 - core), d_r.at[k])
 
-    long.start()
     share_kv(0, 0)
-    wq_ring.forward_left()
-    wq_ring.forward_right()
     wait_for(normed.at[other], n_r.at[1])
     push(normed.at[other], normed.at[other], n_s.at[2], n_r.at[2], sibling)
-    assign_slots(expert_ids, slot_tok, slot_at)
     wait_for(normed.at[x_lo * 2 + 1 - core], n_r.at[0])
     own_wq.wait()
     wq_ring.finish()
+
+    def q_rows(xt, zz):
+        return q_ref.at[xt, pl.ds(zz * 256, 256)]
+
+    def query_part(xt):
+        tokens = normed[pl.ds(xt * 2, 2)].reshape(256, 2048)
+        at = pl.ds(pl.multiple_of(xt * 256, 256), 256)
+        cos, sin = cosine[at, :], sine[at, :]
+        block = jnp.where(xt == 0, ctx, 7 - ctx)
+        for pair in range(2):
+            weights = jnp.concatenate([wq_all[2 * pair], wq_all[2 * pair + 1]], axis=1)
+            raw = jnp.dot(tokens, weights, preferred_element_type=jnp.float32)
+            for k in range(2):
+                zz = 2 * pair + k
+                query = rope(rms_scale(raw[:, k * 128 : (k + 1) * 128], q_gain[...]), cos, sin)
+                q_stage[xt, zz] = query.astype(jnp.bfloat16)
+                is_self = (zz == z) & (xt == 0)
+
+                @pl.when(is_self)
+                def _(zz=zz):
+                    pltpu.make_async_copy(q_stage.at[xt, zz], q_rows(xt, z), q_r.at[xt * 4 + z]).start()
+
+                @pl.when(jnp.logical_not(is_self))
+                def _(zz=zz):
+                    push(
+                        q_stage.at[xt, zz], q_rows(xt, z), q_s.at[xt * 4 + zz], q_r.at[xt * 4 + z],
+                        (block, zz * 4 + x_lo * 2 + core),
+                    )
+
+    query_part(x_lo)
     wait_for(normed.at[(1 - x_lo) * 2 + 1 - core], n_r.at[2])
-
-    def q_rows(zz):
-        return q_ref.at[zz // 2, pl.ds((zz % 2) * 512, 512)]
-
-    tokens = normed[...].reshape(512, 2048)
-    for pair in range(2):
-        weights = jnp.concatenate([wq_all[2 * pair], wq_all[2 * pair + 1]], axis=1)
-        raw = jnp.dot(tokens, weights, preferred_element_type=jnp.float32)
-        for k in range(2):
-            zz = 2 * pair + k
-            query = rope(rms_scale(raw[:, k * 128 : (k + 1) * 128], q_gain[...]), cosine[...], sine[...])
-            q_stage[zz] = query.astype(jnp.bfloat16)
-            is_self = (zz == z) & (z < 2)
-
-            @pl.when(is_self)
-            def _(zz=zz):
-                pltpu.make_async_copy(q_stage.at[zz], q_rows(z), q_r.at[z]).start()
-
-            @pl.when(jnp.logical_not(is_self))
-            def _(zz=zz):
-                push(q_stage.at[zz], q_rows(z), q_s.at[zz], q_r.at[z], (far_ctx, zz * 4 + x_lo * 2 + core))
+    query_part(1 - x_lo)
 
     def shard(dz, xl, cc):
         return w_all.at[(z + dz) % 4, xl, cc]
@@ -328,11 +352,30 @@
     push(w_out, shard(0, x_lo, core), x_s.at[0], x_r.at[0], x_near)
     share(0, w_out)
 
-    def stage_1():
-        long.forward_left()
-        long.forward_right()
+    def kv_forward():
+        for n in (3, 1):
+            columns[n].forward_left()
+            columns[n].forward_right()
+
+    def kv_forward_last():
+        columns[2].forward_left()
         share_kv(1, 3)
+        columns[2].forward_right()
         share_kv(2, 1)
+
+    def kv_left():
+        theirs_kv(1, 3)
+
+    def kv_right():
+        theirs_kv(2, 1)
+
+    def kv_far():
+        for n in (0, 3, 1, 2):
+            columns[n].finish()
+        share_kv(3, 2)
+        theirs_kv(3, 2)
+
+    def w_forward():
         ring.forward_left()
         ring.forward_right()
         share(1)
@@ -342,18 +385,11 @@
         push(theirs, theirs, b_s.at[0], b_r.at[0], z_plus)
         push(theirs, theirs, b_s.at[1], b_r.at[1], z_minus)
         share(4)
-        theirs_kv(1, 3)
-
-    def stage_2():
+
+    def w_far():
         ring.finish()
         push(shard(2, x_lo, core), shard(2, x_lo, core), x_s.at[1], x_r.at[1], x_near)
         share(3)
-        theirs_kv(2, 1)
-
-    def stage_3():
-        long.finish()
-        share_kv(3, 2)
-        theirs_kv(3, 2)
 
     def stage_4():
         wait_for(shard(3, 1 - x_lo, core), b_r.at[0])
@@ -365,12 +401,13 @@
 
     scale = math.log2(math.e) / math.sqrt(128)
 
-    def step(q, k, v, m_prev, acc, first_row):
+    def step(q, k, v, m_prev, acc, masked):
         s = lax.dot_general(q, k, (((1,), (1,)), ((), ())), preferred_element_type=jnp.float32)
-        if first_row is not None:
-            row = lax.broadcasted_iota(jnp.int32, s.shape, 0) + first_row
-            col = lax.broadcasted_iota(jnp.int32, s.shape, 1)
-            s = jnp.where(col <= row, s, -1e30)
+        if masked:
+            row = lax.broadcasted_iota(jnp.int32, (DB, DB), 0)
+            col = lax.broadcasted_iota(jnp.int32, (DB, DB), 1)
+            edge = jnp.where(col <= row, s[:, -DB:], -1e30)
+            s = edge if s.shape[1] == DB else jnp.concatenate([s[:, :-DB], edge], axis=1)
         m_new = jnp.maximum(m_prev, jnp.max(s, axis=1, keepdims=True))
         alpha = jnp.exp2((m_prev - m_new) * scale)
         shift = (m_new * scale)[:, :1]
@@ -381,7 +418,7 @@
 
     m_scr[...] = jnp.full_like(m_scr, -1e30)
     acc_scr[...] = jnp.zeros_like(acc_scr)
-    last = (2 * ctx, 15 - 2 * ctx)
+    last = (2 * ctx, 14 - 2 * ctx)
 
     def tile_of(t):
         at = (t // 8, (t // 2) % 4, pl.ds((t % 2) * 2, 2))
@@ -391,44 +428,48 @@
         k, v = tile_of(t)
         for b in range(1024 // QB):
             rows = pl.ds(b * QB, QB)
-            m, a = step(q_ref[half, rows, :], k, v, m_scr[half, rows, :], acc_scr[half, rows, :], None)
+            m, a = step(q_ref[half, rows, :], k, v, m_scr[half, rows, :], acc_scr[half, rows, :], False)
             m_scr[half, rows, :] = m
             acc_scr[half, rows, :] = a
 
-    for zz in range(4):
-        wait_for(q_rows(zz), q_r.at[zz])
+    assign_slots(expert_ids, slot_tok, slot_at)
     theirs_kv(0, 0)
-
-    def visit(s, carry):
-        pl.when(s == 1)(stage_1)
-        pl.when(s == 2)(stage_2)
-        pl.when(s == 3)(stage_3)
+    for xt in range(2):
+        for zz in range(4):
+            wait_for(q_rows(xt, zz), q_r.at[xt * 4 + zz])
+
+    def visit(i, carry):
+        for at, act in (
+            (1, kv_forward), (3, kv_forward_last), (4, kv_left), (6, w_forward), (8, kv_right), (11, w_far), (12, kv_far)
+        ):
+            pl.when(i == at)(act)
+        s = i // 4
         n = jnp.where(s == 1, 3, jnp.where(s == 2, 1, jnp.where(s == 3, 2, 0)))
-        yy = (y + n) % 4
-
-        def one(u, carry):
-            t = ((u // 4) * 4 + yy) * 2 + (u // 2) % 2
-            half = u % 2
+        t = (((i // 2) % 2) * 4 + (y + n) % 4) * 2 + i % 2
+
+        def one(half, carry):
             pl.when(t < jnp.where(half == 0, last[0], last[1]))(functools.partial(full, half, t))
             return carry
 
-        return lax.fori_loop(0, 8, one, carry)
-
-    lax.fori_loop(0, 4, visit, 0)
+        return lax.fori_loop(0, 2, one, carry)
+
+    lax.fori_loop(0, 16, visit, 0)
     stage_4()
     my_columns = pl.ds(pl.multiple_of(exp * 128, 128), 128)
     for half in range(2):
-        k, v = tile_of(last[half])
-        for b in range(1024 // DB):
-            rows = pl.ds(b * DB, DB)
-            seen = (b + 1) * DB
+        block = ctx if half == 0 else 7 - ctx
+        k = kv[0, block // 4, block % 4].reshape(2048, 128)
+        v = kv[1, block // 4, block % 4].reshape(2048, 128)
+        for zz in range(4):
+            rows = pl.ds(zz * DB, DB)
+            seen = zz * 512 + half * 256 + DB
             m, a = step(
-                q_ref[half, rows, :], k[:seen], v[:seen], m_scr[half, rows, :], acc_scr[half, rows, :], b * DB
+                q_ref[half, rows, :], k[:seen], v[:seen], m_scr[half, rows, :], acc_scr[half, rows, :], True
             )
             o_ref[half, rows, :] = (a[:, :128] / a[:, 128:]).astype(jnp.bfloat16)
             for i in range(2):
-                e = half * 8 + b * 2 + i
-                src = o_ref.at[half, pl.ds(b * DB + i * 128, 128)]
+                e = zz * 4 + half * 2 + i
+                src = o_ref.at[half, pl.ds(zz * DB + i * 128, 128)]
                 dst = heads.at[:, my_columns]
                 if half:
                     push(src, dst, h_s, h_r, (7 - ctx, e))
@@ -443,7 +484,8 @@
     ring.drain()
     for sem in (x_s.at[0], x_s.at[1], b_s.at[0], b_s.at[1]):
         wait_for(w_out, sem)
-    long.drain()
+    for n in range(4):
+        columns[n].drain()
     for k, n in enumerate((0, 3, 1, 2)):
         wait_for(mine_of(n), d_s.at[k])
     wq_ring.drain()
@@ -453,9 +495,11 @@
     wait_for(normed.at[other], n_s.at[2])
     for zz in range(4):
 
-        @pl.when(jnp.logical_not((zz == z) & (z < 2)))
+        wait_for(q_stage.at[1, zz], q_s.at[4 + zz])
+
+        @pl.when(zz != z)
         def _(zz=zz):
-            wait_for(q_stage.at[zz], q_s.at[zz])
+            wait_for(q_stage.at[0, zz], q_s.at[zz])
 
         for which in range(2):
 
@@ -465,11 +509,11 @@
 
     wait_for(heads, h_r)
 
-    @pl.when(exp < 8)
+    @pl.when(x_lo == 0)
     def _():
         wait_for(heads.at[:, pl.ds(0, 15 * 128)], h_s)
 
-    @pl.when(exp >= 8)
+    @pl.when(x_lo == 1)
     def _():
         wait_for(heads, h_s)
 
@@ -503,13 +547,13 @@
             pltpu.VMEM((4, 2048, 128), low),
             pltpu.VMEM((4, 128, 2048), low),
             pltpu.VMEM((2, 2, 128, 128), low),
-            pltpu.VMEM((4, 512, 128), low),
+            pltpu.VMEM((2, 4, 256, 128), low),
             pltpu.VMEM((2, 1024, 128), low),
             pltpu.VMEM((2, 1024, 128), low),
             pltpu.VMEM((2, 1024, 128), f32),
             pltpu.VMEM((2, 1024, 256), f32),
             dma((9,)), dma, dma((4,)), dma((4,)), dma((3,)), dma((3,)), dma((8,)), dma((8,)),
-            dma((4,)), dma((4,)), dma((4,)), dma((4,)), dma((4,)), dma((4,)), dma((4,)), dma((4,)),
+            dma((4,)), dma((4,)), dma((16,)), dma((16,)), dma((4,)), dma((4,)), dma((8,)), dma((8,)),
             dma, dma((4,)), dma((4,)), dma((2,)), dma((2,)), dma((2,)), dma((2,)), dma((8,)), dma((8,)), dma, dma,
         ],
         compiler_params=pltpu.CompilerParams(

time: 265 us -> 271 us (1.023)
  Pallas kernels: 259 us -> 262 us
    pallas_call x1, Pallas kernels: 150 us -> 164 us  [tail(): pl.pallas_call(functools.partial(moe_kernel, CAP), out_shape=jax.ShapeDty...]
    pallas_call x1, Pallas kernels: 109 us -> 98.4 us  [attend(): pl.pallas_call(attend_kernel, out_shape=(jax.ShapeDtypeStruct((128, 2048)...]
where the time goes in v5:
time: 271 us; the launch traced here: 267 us
  Pallas kernels  262 us (97%)
    pallas_call x1, Pallas kernels, tail(): pl.pallas_call(functools.partial(moe_kernel, CAP), out_shape=jax.ShapeDty...  164 us
    pallas_call x1, Pallas kernels, attend(): pl.pallas_call(attend_kernel, out_shape=(jax.ShapeDtypeStruct((128, 2048)...  98.4 us

profile of v5, /device:TPU:0, one launch (start us, length us, event | category | flops | bytes accessed | tf_op | source)
XLA Modules:
  0.0 267.0 jit_solution(12278511313470440997)
XLA Ops:
  0.0 0.0 copy-start
  0.0 1.0 fusion
  1.0 1.0 pad_maximum_fusion
  2.0 98.4 %attend.1 = (bf16[128,2048]{1,0:T(8,128)(2,1)}, bf16[4,2,2,128,2048]{4,3,2,1,0:T(8,128)(2,1)}, s32[16,128]{1,0:T(8,128)}, s32[128,8]{1,0:T(8,128)}) custom-call(bf16[128,2048]{1,0:T(8,128)(2,1)} %hidden_in.3, f32[1,2048]{1,0:T(1,128)} %bitcast.13, bf16[2048,128]{1,0:T(8,128)(2,1)} %wq.1, bf16[2048,256]{1,0:T(8,128)(2,1)} %wk_in.1, bf16[2048,256]{1,0:T(8,128)(2,1)} %wv_in.1, ...), custom_call_target="tpu_custom_call" | custom-call | tf_op jit(solution)/shard_map/attend/pallas_call | solution.py:526
  100.4 0.0 copy-done
  100.4 0.7 copy.15.gates_in
  101.2 163.8 %tail.1 = bf16[128,2048]{1,0:T(8,128)(2,1)} custom-call(s32[16,128]{1,0:T(8,128)} %get-tuple-element.9.slot_tok, bf16[128,2048]{1,0:T(8,128)(2,1)} %get-tuple-element.10.heads_in, bf16[128,2048]{1,0:T(8,128)(2,1)} %hidden_in.3, f32[1,2048]{1,0:T(1,128)} %bitcast.14, s32[128,8]{1,0:T(8,128)} %get-tuple-element.11.slot_in, f32[128,8]{1,0:T(8,128)} %copy.15.gates_in, ...), custom_call_target="tpu_custom_call" | custom-call | tf_op jit(solution)/shard_map/tail/pallas_call | solution.py:711
  264.9 1.9 copy.17
  (2 shorter events, 0.0 us)
Async XLA Ops:
  0.0 100.4 %copy-start = (f32[128,8]{0,1:T(8,128)S(1)}, f32[128,8]{0,1:T(8,128)}, u32[]{:S(2)}) copy-start(f32[128,8]{0,1:T(8,128)} %param.27) | copy-start | bytes 12292

commit v6 on v5

--- a/solution.py
+++ b/solution.py
@@ -28,7 +28,7 @@
 
 def offset_parts(o):
     dc, k, dy, dx = o // 64, (o // 16) % 4, (o // 4) % 4, o % 4
-    return dx, dy, (k + 8 - dx - dy) % 4, dc
+    return dx, (dy + dx) % 4, (k + 12 - 2 * dx - dy) % 4, dc
 
 
 def peer_to(o):
@@ -49,7 +49,7 @@
     dy = ((e >> 4) + 4 - y) & 3
     dz = ((e >> 2) + 4 - z) & 3
     dc = (e + 2 - c) & 1
-    return dc * 64 + ((dx + dy + dz) & 3) * 16 + dy * 4 + dx
+    return dc * 64 + ((dx + dy + dz) & 3) * 16 + ((dy - dx) & 3) * 4 + dx
 epsilon = 1e-06
 rope_base = 1000000.0
 
@@ -440,7 +440,7 @@
 
     def visit(i, carry):
         for at, act in (
-            (1, kv_forward), (3, kv_forward_last), (4, kv_left), (6, w_forward), (8, kv_right), (11, w_far), (12, kv_far)
+            (1, kv_forward), (3, kv_forward_last), (4, kv_left), (4, w_forward), (8, kv_right), (8, w_far), (12, kv_far)
         ):
             pl.when(i == at)(act)
         s = i // 4

time: 271 us -> 269 us (level)
  the two profiles are of different devices: /device:TPU:0 before, /device:TPU:19 now
where the time goes in v6:
time: 269 us; the launch traced here: 265 us
  Pallas kernels  260 us (97%)
    pallas_call x1, Pallas kernels, tail(): pl.pallas_call(functools.partial(moe_kernel, CAP), out_shape=jax.ShapeDty...  164 us
    pallas_call x1, Pallas kernels, attend(): pl.pallas_call(attend_kernel, out_shape=(jax.ShapeDtypeStruct((128, 2048)...  96.9 us

profile of v6, /device:TPU:19, one launch (start us, length us, event | category | flops | bytes accessed | tf_op | source)
XLA Modules:
  0.0 265.3 jit_solution(2944991599521876501)
XLA Ops:
  0.0 0.0 copy-start
  0.0 1.0 fusion
  1.0 1.0 pad_maximum_fusion
  2.0 96.9 %attend.1 = (bf16[128,2048]{1,0:T(8,128)(2,1)}, bf16[4,2,2,128,2048]{4,3,2,1,0:T(8,128)(2,1)}, s32[16,128]{1,0:T(8,128)}, s32[128,8]{1,0:T(8,128)}) custom-call(bf16[128,2048]{1,0:T(8,128)(2,1)} %hidden_in.3, f32[1,2048]{1,0:T(1,128)} %bitcast.13, bf16[2048,128]{1,0:T(8,128)(2,1)} %wq.1, bf16[2048,256]{1,0:T(8,128)(2,1)} %wk_in.1, bf16[2048,256]{1,0:T(8,128)(2,1)} %wv_in.1, ...), custom_call_target="tpu_custom_call" | custom-call | tf_op jit(solution)/shard_map/attend/pallas_call | solution.py:526
  98.9 0.0 copy-done
  98.9 0.7 copy.15.gates_in
  99.7 163.5 %tail.1 = bf16[128,2048]{1,0:T(8,128)(2,1)} custom-call(s32[16,128]{1,0:T(8,128)} %get-tuple-element.9.slot_tok, bf16[128,2048]{1,0:T(8,128)(2,1)} %get-tuple-element.10.heads_in, bf16[128,2048]{1,0:T(8,128)(2,1)} %hidden_in.3, f32[1,2048]{1,0:T(1,128)} %bitcast.14, s32[128,8]{1,0:T(8,128)} %get-tuple-element.11.slot_in, f32[128,8]{1,0:T(8,128)} %copy.15.gates_in, ...), custom_call_target="tpu_custom_call" | custom-call | tf_op jit(solution)/shard_map/tail/pallas_call | solution.py:711
  263.2 1.9 copy.17
  (2 shorter events, 0.0 us)
Async XLA Ops:
  0.0 98.9 %copy-start = (f32[128,8]{0,1:T(8,128)S(1)}, f32[128,8]{0,1:T(8,128)}, u32[]{:S(2)}) copy-start(f32[128,8]{0,1:T(8,128)} %param.27) | copy-start | bytes 12292

commit v7 on v6

--- a/solution.py
+++ b/solution.py
@@ -598,12 +598,12 @@
         pl.semaphore_signal(barrier, inc=1, device_id=peer_to(o), device_id_type=MESH)
         return carry
 
-    lax.fori_loop(1, GROUPS * PEERS, greet, 0)
     x_tiles[tok:] = jnp.zeros((8, 16, 128), jnp.bfloat16)
     for load in loads:
         load.wait()
     projected = jnp.dot(heads[...], vo[...], preferred_element_type=jnp.float32)
     summed = (hidden[...].astype(jnp.float32) + projected).astype(jnp.bfloat16)
+    lax.fori_loop(1, GROUPS * PEERS, greet, 0)
     resid[...] = summed
     normed = rms_scale(summed.astype(jnp.float32), ffn_gain[...])
     for s in range(16):
@@ -678,7 +678,7 @@
         ans_buf[pl.ds(g * PEERS, PEERS)] = answers
         lax.fori_loop(g * PEERS + first, (g + 1) * PEERS, lambda o, c, g=g: start_back(o, g), g)
     acc[...] = resid[...].astype(jnp.float32)
-    weights = gates[...]
+    weights = gates[...].T
     shares = weights / jnp.sum(weights, axis=1, keepdims=True)
     at = slot_at[...]
     for g in range(GROUPS):
@@ -728,7 +728,7 @@
             pltpu.VMEM((tok, width), low),
             pltpu.VMEM((1, width), f32),
             pltpu.VMEM((tok, TOPK), jnp.int32),
-            pltpu.VMEM((tok, TOPK), f32),
+            pltpu.VMEM((TOPK, tok), f32),
             dma((3,)), dma((6,)), dma((GROUPS,)), dma((GROUPS,)), dma((GROUPS,)), dma((GROUPS,)),
         ],
         compiler_params=pltpu.CompilerParams(
@@ -752,7 +752,7 @@
         jnp.concatenate([cosine, cosine], axis=1), jnp.concatenate([-sine, sine], axis=1), expert_ids.T, w_out,
     )
     return tail(
-        heads, hidden_in, ffn_gain, w_out_all.reshape(2048, 2048), slot_tok, slot_at, gate_weights,
+        heads, hidden_in, ffn_gain, w_out_all.reshape(2048, 2048), slot_tok, slot_at, gate_weights.T,
         w_gate[0], w_up[0], w_down[0],
     )
 

time: 269 us -> 273 us (1.015)
  the two profiles are of different devices: /device:TPU:19 before, /device:TPU:23 now
where the time goes in v7:
time: 273 us; the launch traced here: 269 us
  Pallas kernels  265 us (97%)
    pallas_call x1, Pallas kernels, tail(): pl.pallas_call(functools.partial(moe_kernel, CAP), out_shape=jax.ShapeDty...  172 us
    pallas_call x1, Pallas kernels, attend(): pl.pallas_call(attend_kernel, out_shape=(jax.ShapeDtypeStruct((128, 2048)...  92.7 us

profile of v7, /device:TPU:23, one launch (start us, length us, event | category | flops | bytes accessed | tf_op | source)
XLA Modules:
  0.0 268.7 jit_solution(14711235748007708306)
XLA Ops:
  0.0 1.0 fusion
  1.0 1.0 pad_maximum_fusion
  2.0 92.7 %attend.1 = (bf16[128,2048]{1,0:T(8,128)(2,1)}, bf16[4,2,2,128,2048]{4,3,2,1,0:T(8,128)(2,1)}, s32[16,128]{1,0:T(8,128)}, s32[128,8]{1,0:T(8,128)}) custom-call(bf16[128,2048]{1,0:T(8,128)(2,1)} %hidden_in.3, f32[1,2048]{1,0:T(1,128)} %bitcast.14, bf16[2048,128]{1,0:T(8,128)(2,1)} %wq.1, bf16[2048,256]{1,0:T(8,128)(2,1)} %wk_in.1, bf16[2048,256]{1,0:T(8,128)(2,1)} %wv_in.1, ...), custom_call_target="tpu_custom_call" | custom-call | tf_op jit(solution)/shard_map/attend/pallas_call | solution.py:526
  94.8 171.8 %tail.1 = bf16[128,2048]{1,0:T(8,128)(2,1)} custom-call(s32[16,128]{1,0:T(8,128)} %get-tuple-element.9.slot_tok, bf16[128,2048]{1,0:T(8,128)(2,1)} %get-tuple-element.10.heads_in, bf16[128,2048]{1,0:T(8,128)(2,1)} %hidden_in.3, f32[1,2048]{1,0:T(1,128)} %bitcast.15, s32[128,8]{1,0:T(8,128)} %get-tuple-element.11.slot_in, f32[8,128]{1,0:T(8,128)} %bitcast.16, ...), custom_call_target="tpu_custom_call" | custom-call | tf_op jit(solution)/shard_map/tail/pallas_call | solution.py:711
  266.5 1.9 copy.16
  (2 shorter events, 0.0 us)

commit v8 on v4

--- a/solution.py
+++ b/solution.py
@@ -28,7 +28,7 @@
 
 def offset_parts(o):
     dc, k, dy, dx = o // 64, (o // 16) % 4, (o // 4) % 4, o % 4
-    return dx, dy, (k + 8 - dx - dy) % 4, dc
+    return dx, (dy + dx) % 4, (k + 12 - 2 * dx - dy) % 4, dc
 
 
 def peer_to(o):
@@ -49,7 +49,7 @@
     dy = ((e >> 4) + 4 - y) & 3
     dz = ((e >> 2) + 4 - z) & 3
     dc = (e + 2 - c) & 1
-    return dc * 64 + ((dx + dy + dz) & 3) * 16 + dy * 4 + dx
+    return dc * 64 + ((dx + dy + dz) & 3) * 16 + ((dy - dx) & 3) * 4 + dx
 epsilon = 1e-06
 rope_base = 1000000.0
 
@@ -634,7 +634,7 @@
         ans_buf[pl.ds(g * PEERS, PEERS)] = answers
         lax.fori_loop(g * PEERS + first, (g + 1) * PEERS, lambda o, c, g=g: start_back(o, g), g)
     acc[...] = resid[...].astype(jnp.float32)
-    weights = gates[...]
+    weights = gates[...].T
     shares = weights / jnp.sum(weights, axis=1, keepdims=True)
     at = slot_at[...]
     for g in range(GROUPS):
@@ -684,7 +684,7 @@
             pltpu.VMEM((tok, width), low),
             pltpu.VMEM((1, width), f32),
             pltpu.VMEM((tok, TOPK), jnp.int32),
-            pltpu.VMEM((tok, TOPK), f32),
+            pltpu.VMEM((TOPK, tok), f32),
             dma((3,)), dma((6,)), dma((GROUPS,)), dma((GROUPS,)), dma((GROUPS,)), dma((GROUPS,)),
         ],
         compiler_params=pltpu.CompilerParams(
@@ -708,7 +708,7 @@
         jnp.concatenate([cosine, cosine], axis=1), jnp.concatenate([-sine, sine], axis=1), expert_ids.T, w_out,
     )
     return tail(
-        heads, hidden_in, ffn_gain, w_out_all.reshape(2048, 2048), slot_tok, slot_at, gate_weights,
+        heads, hidden_in, ffn_gain, w_out_all.reshape(2048, 2048), slot_tok, slot_at, gate_weights.T,
         w_gate[0], w_up[0], w_down[0],
     )
 

time: 265 us -> 271 us (1.023)
  Pallas kernels: 259 us -> 264 us
    pallas_call x1, Pallas kernels: 150 us -> 155 us  [tail(): pl.pallas_call(functools.partial(moe_kernel, CAP), out_shape=jax.ShapeDty...]
where the time goes in v8:
time: 271 us; the launch traced here: 268 us
  Pallas kernels  264 us (97%)
    pallas_call x1, Pallas kernels, tail(): pl.pallas_call(functools.partial(moe_kernel, CAP), out_shape=jax.ShapeDty...  155 us
    pallas_call x1, Pallas kernels, attend(): pl.pallas_call(attend_kernel, out_shape=(jax.ShapeDtypeStruct((128, 2048)...  109 us

profile of v8, /device:TPU:0, one launch (start us, length us, event | category | flops | bytes accessed | tf_op | source)
XLA Modules:
  0.0 267.8 jit_solution(15369217505848971889)
XLA Ops:
  0.0 1.0 fusion
  1.0 1.0 pad_maximum_fusion
  2.0 108.7 %attend.1 = (bf16[128,2048]{1,0:T(8,128)(2,1)}, bf16[4,2,2,128,2048]{4,3,2,1,0:T(8,128)(2,1)}, s32[16,128]{1,0:T(8,128)}, s32[128,8]{1,0:T(8,128)}) custom-call(bf16[128,2048]{1,0:T(8,128)(2,1)} %hidden_in.3, f32[1,2048]{1,0:T(1,128)} %bitcast.14, bf16[2048,128]{1,0:T(8,128)(2,1)} %wq.1, bf16[2048,256]{1,0:T(8,128)(2,1)} %wk_in.1, bf16[2048,256]{1,0:T(8,128)(2,1)} %wv_in.1, ...), custom_call_target="tpu_custom_call" | custom-call | tf_op jit(solution)/shard_map/attend/pallas_call | solution.py:482
  110.7 155.2 %tail.1 = bf16[128,2048]{1,0:T(8,128)(2,1)} custom-call(s32[16,128]{1,0:T(8,128)} %get-tuple-element.9.slot_tok, bf16[128,2048]{1,0:T(8,128)(2,1)} %get-tuple-element.10.heads_in, bf16[128,2048]{1,0:T(8,128)(2,1)} %hidden_in.3, f32[1,2048]{1,0:T(1,128)} %bitcast.15, s32[128,8]{1,0:T(8,128)} %get-tuple-element.11.slot_in, f32[8,128]{1,0:T(8,128)} %bitcast.16, ...), custom_call_target="tpu_custom_call" | custom-call | tf_op jit(solution)/shard_map/tail/pallas_call | solution.py:667
  265.9 1.9 copy.16
  (2 shorter events, 0.0 us)
